TPU v7x, 32 devices: a whole 2x2x4 slice. The times are simulated.
32 devices in a mesh: pair: 2 (over y), section: 4 (over z), dp: 4 (over x, core).
Axes of the slice: x: 2, y: 2, z: 4, core: 2. Of those that a mesh axis runs over, the one named last changes fastest.
Arguments:
- grads: float32 [8, 4, 8, 7168], P(('section', 'pair'), 'dp'), parts along dimension 0, may hold values from -6 to 6
- master: float32 [32, 7168], P(('section', 'pair', 'dp')), parts along dimension 0, may hold values from -6 to 6
- moment: float32 [32, 7168], P(('section', 'pair', 'dp')), parts along dimension 0, may hold values from -12 to 12
- second: float32 [32, 7168], P(('section', 'pair', 'dp')), parts along dimension 0, may hold values from 0.5 to 50
- step: int32 [4], P('section'), parts along dimension 0, may hold values from 1 to 8
Outputs:
- new_master: float32 [32, 7168], P(('section', 'pair', 'dp')), parts along dimension 0
- new_moment: float32 [32, 7168], P(('section', 'pair', 'dp')), parts along dimension 0
- new_second: float32 [32, 7168], P(('section', 'pair', 'dp')), parts along dimension 0
- params: bfloat16 [32, 7168], P('section'), parts along dimension 0
There are 4 independent parts, one for each index of `section`. A program takes and returns all parts, laid end to end along the dimension named above; each array names one. Nothing has to cross between parts.
All inputs are finite; a program needn't handle non-finite values.
Results may differ from a plain program's by a relative error of at most 0.0004.
Values may be sent and summed in bfloat16 or wider, within the bound.
No kernel may reach another device: no remote copies, remote signals or barrier semaphores. Data moves between devices by JAX's collectives and lax.ppermute only.
A program may use at most 64 MiB of HBM per device.

v0:
```python
import functools
import math

import jax
import jax.numpy as jnp
from jax import lax
from jax.experimental import pallas as pl
from jax.experimental.pallas import tpu as pltpu
from jax.sharding import PartitionSpec as P

GROUP = ("pair", "dp")
LANES = 128


def swap(array, bit):
    size = lax.axis_size(GROUP)
    return lax.ppermute(array, GROUP, [(i, i ^ bit) for i in range(size)])


def row_at(row, tiles, rows):
    sub = min(8, rows)
    return pl.ds((row // sub) * (tiles * sub) + row % sub, tiles, stride=sub)


def pick_kernel(pairs, shards, own, tiles, *refs):
    source_ref, added, (keep_ref, give_ref) = refs[0], refs[1:-2], refs[-2:]
    shard = lax.axis_index("dp")
    core, near = shard & 1, shard & 2
    rows = pairs * shards * own
    slot = 0
    for pair in range(pairs):
        for far in range(shards // 4):
            for o in range(own):
                to = slice(slot * tiles, (slot + 1) * tiles)
                for i, (out_ref, bit) in enumerate(((keep_ref, near), (give_ref, 2 - near))):
                    row = (pair * shards + far * 4 + bit + core) * own + o
                    picked = source_ref[row_at(row, tiles, rows), :]
                    out_ref[to, :] = picked + added[i][to, :] if added else picked
                slot += 1


def adam(total, master, moment, second, count):
    new_moment = 0.9 * moment + 0.1 * total
    new_second = 0.95 * second + 0.05 * total * total
    first_fix = 1.0 - jnp.exp(count * jnp.log(jnp.full_like(count, 0.9)))
    second_fix = 1.0 - jnp.exp(count * jnp.log(jnp.full_like(count, 0.95)))
    update = new_moment / first_fix / (jnp.sqrt(new_second / second_fix) + 1e-08) + 0.1 * master
    return master - 0.03 * update, new_moment, new_second


def totals(size, sums):
    keep, near, level, cross = (s[...] for s in sums)
    both = (keep + near) + (level + cross)
    first = lax.axis_index("pair") == 0
    low, high = both[:size], both[size:]
    return jnp.where(first, low, high), jnp.where(first, high, low)


def params_kernel(size, step_ref, keep, near, level, cross, master, moment, second, state, out_ref):
    count = jnp.full((1, LANES), step_ref[0], jnp.int32).astype(jnp.float32)
    mine, theirs = totals(size, (keep, near, level, cross))
    a, _, _ = adam(mine, master[...], moment[...], second[...], count)
    b, _, _ = adam(theirs, state[:size], state[size:2 * size], state[2 * size:], count)
    out_ref[...] = jnp.concatenate([a, b], axis=0).astype(out_ref.dtype)


def own_kernel(size, step_ref, keep, near, level, cross, master, moment, second, m_ref, v_ref, s_ref):
    count = jnp.full((1, LANES), step_ref[0], jnp.int32).astype(jnp.float32)
    mine, _ = totals(size, (keep, near, level, cross))
    m_ref[...], v_ref[...], s_ref[...] = adam(mine, master[...], moment[...], second[...], count)


def order_kernel(pairs, shards, own, tiles, *refs):
    pieces, out_ref, scratch = refs[:4], refs[4], refs[5]
    pair, shard = lax.axis_index("pair"), lax.axis_index("dp") & 3
    rows = pairs * 4 * own
    for k in range(4):
        piece = pieces[k][...].astype(jnp.float32)
        for s in range(pairs):
            for o in range(own):
                row = ((pair ^ s) * 4 + (shard ^ k)) * own + o
                start = (s * own + o) * tiles
                scratch[row_at(row, tiles, rows), :] = piece[start:start + tiles]
    out_ref[...] = scratch[...].astype(out_ref.dtype)


def call(body, outs, *args, scratch=()):
    held = sum(math.prod(a.shape) * a.dtype.itemsize for a in [*args, *jax.tree.leaves(outs)])
    specs = [pl.BlockSpec(memory_space=pltpu.SMEM if a.dtype == jnp.int32 else pltpu.VMEM) for a in args]
    return pl.pallas_call(
        body,
        out_shape=outs,
        in_specs=specs,
        out_specs=jax.tree.map(lambda _: pl.BlockSpec(memory_space=pltpu.VMEM), outs),
        scratch_shapes=list(scratch),
        compiler_params=pltpu.CompilerParams(vmem_limit_bytes=4 * held + (1 << 20)),
    )(*args)


def per_device(grads, master, moment, second, step):
    rows, width = grads.shape[2], grads.shape[3]
    own, tiles = master.shape[0], width // LANES
    pairs, shards = lax.axis_size("pair"), lax.axis_size("dp")
    shard = lax.axis_index("dp")
    far = [1 << b for b in range(2, (shards - 1).bit_length())]
    size, f32 = own * tiles, jnp.float32
    shaped = jax.ShapeDtypeStruct

    master, moment, second = (a.reshape(size, LANES) for a in (master, moment, second))
    sub = min(8, rows)
    local = grads.reshape(rows // sub, sub, tiles, LANES).transpose(0, 2, 1, 3).reshape(rows * tiles, LANES)

    theirs = swap(local, 1)
    state = swap(jnp.concatenate([master, moment, second], axis=0), shards)
    half = shaped((pairs * (shards // 4) * size, LANES), f32)
    pick = functools.partial(pick_kernel, pairs, shards, own, tiles)
    mine = call(pick, (half, half), local)
    keep, give = call(pick, (half, half), theirs, *mine)

    for bit in reversed(far):
        low = (shard & bit) == 0
        held = jnp.stack([keep, give]).reshape(2, pairs, 2, -1, LANES)
        mine = jnp.where(low, held[:, :, 0], held[:, :, 1])
        other = jnp.where(low, held[:, :, 1], held[:, :, 0])
        keep, give = (mine + swap(other, bit)).reshape(2, -1, LANES)

    near, cross = swap(give, 2), swap(give, shards | 2)
    level = swap(keep, shards)
    sums = (keep, near, level, cross)

    params = call(
        functools.partial(params_kernel, size), shaped((pairs * size, LANES), jnp.bfloat16),
        step, *sums, master, moment, second, state)
    row = shaped((size, LANES), f32)
    news = call(
        functools.partial(own_kernel, size), (row, row, row), step, *sums, master, moment, second)

    pieces = [params, swap(params, 1), swap(params, 2), swap(params, 3)]
    block = pairs * 4 * size
    params = call(
        functools.partial(order_kernel, pairs, shards, own, tiles), shaped((block, LANES), jnp.bfloat16),
        *pieces, scratch=[pltpu.VMEM((block, LANES), f32)])
    near_rows = pairs * 4 * own
    sub = min(8, near_rows)
    params = params.reshape(near_rows // sub, tiles, sub, LANES).transpose(0, 2, 1, 3)
    params = params.reshape(pairs, 4 * own, width)
    for bit in far:
        low, got = (shard & bit) == 0, swap(params, bit)
        params = jnp.concatenate([jnp.where(low, params, got), jnp.where(low, got, params)], axis=1)
    return tuple(n.reshape(own, width) for n in news) + (params.reshape(rows, width),)


def solution(mesh):
    placed = (
        P(("section", "pair"), "dp", None, None),
        P(("section", "pair", "dp"), None),
        P(("section", "pair", "dp"), None),
        P(("section", "pair", "dp"), None),
        P("section"),
    )
    return jax.shard_map(
        per_device,
        mesh=mesh,
        in_specs=placed,
        out_specs=(
            P(("section", "pair", "dp"), None),
            P(("section", "pair", "dp"), None),
            P(("section", "pair", "dp"), None),
            P("section", None),
        ),
        check_vma=False,
    )
```

profile of v0, /device:TPU:0, one launch (start us, length us, event | category | flops | bytes accessed | tf_op | source)
XLA Modules:
  0.0 17.8 jit_solution(9239575054536351402)
XLA Ops:
  0.6 0.5 %collective-permute-start = (f32[448,128]{1,0:T(8,128)}, f32[448,128]{1,0:T(8,128)S(1)}, u32[]{:S(2)}, u32[]{:S(2)}) collective-permute-start(f32[448,128]{1,0:T(8,128)} %bitcast.25), channel_id=1, source_target_pairs={{0,1},{1,0},{2,3},{3,2},{16,17},{17,16},{18,19},{19,18},{4,5},{5,4... | collective-permute-start | bytes 688136 | tf_op jit(solution)/shard_map/ppermute | solution.py:17
  1.1 0.8 %pad_maximum_fusion = f32[168,128]{1,0:T(8,128)S(1)} fusion(f32[56,128]{1,0:T(8,128)} %bitcast.22, f32[56,128]{1,0:T(8,128)} %bitcast.19, f32[56,128]{1,0:T(8,128)} %bitcast.16), kind=kLoop, calls=%fused_computation | loop fusion | flops 43008 | bytes 172032 | tf_op jit(solution)/shard_map/concatenate | solution.py:114
  1.9 2.5 %collective-permute-start.4 = (f32[168,128]{1,0:T(8,128)S(1)}, f32[168,128]{1,0:T(8,128)S(1)}, u32[]{:S(2)}, u32[]{:S(2)}) collective-permute-start(f32[168,128]{1,0:T(8,128)S(1)} %pad_maximum_fusion), channel_id=1, source_target_pairs={{0,16},{1,17},{2,18},{3,19},{16,0},{17,1},{18,2},{19,3},{4,20},{5,... | collective-permute-start | bytes 258056 | tf_op jit(solution)/shard_map/ppermute | solution.py:17
  4.5 0.0 copy-start.3
  4.5 0.9 %copy-done.3 = f32[1,1,8,7168]{3,2,1,0:T(8,128)S(1)} copy-done((f32[1,1,8,7168]{3,2,1,0:T(8,128)S(1)}, f32[1,1,8,7168]{3,2,1,0:T(8,128)}, u32[]{:S(2)}) %copy-start.3) | copy-done | bytes 229400
  5.4 0.0 collective-permute-done.refs_0_
  5.5 0.0 copy-start
  5.5 0.0 copy-start.1
  5.5 0.0 copy-start.2
  5.5 0.1 shard_map.85
  5.5 0.1 collective-permute-start.2
  5.6 2.0 %collective-permute-start.1 = (f32[112,128]{1,0:T(8,128)S(1)}, f32[112,128]{1,0:T(8,128)S(1)}, u32[]{:S(2)}, u32[]{:S(2)}) collective-permute-start(f32[112,128]{1,0:T(8,128)S(1)} %get-tuple-element.14), channel_id=1, source_target_pairs={{0,2},{1,3},{2,0},{3,1},{16,18},{17,19},{18,16},{19,17},{4,6},{5,7... | collective-permute-start | bytes 172040 | tf_op jit(solution)/shard_map/ppermute | solution.py:17
  7.6 1.5 %collective-permute-start.3 = (f32[112,128]{1,0:T(8,128)S(1)}, f32[112,128]{1,0:T(8,128)S(1)}, u32[]{:S(2)}, u32[]{:S(2)}) collective-permute-start(f32[112,128]{1,0:T(8,128)S(1)} %get-tuple-element.14), channel_id=1, source_target_pairs={{0,18},{1,19},{2,16},{3,17},{16,2},{17,3},{18,0},{19,1},{4,22},{5,... | collective-permute-start | bytes 172040 | tf_op jit(solution)/shard_map/ppermute | solution.py:17
  9.8 0.0 collective-permute-done.4.state
  9.8 0.0 collective-permute-done.2.level
  9.8 0.1 collective-permute-done.1.near
  9.9 2.8 %collective-permute-done.3.cross = f32[112,128]{1,0:T(8,128)S(1)} collective-permute-done((f32[112,128]{1,0:T(8,128)S(1)}, f32[112,128]{1,0:T(8,128)S(1)}, u32[]{:S(2)}, u32[]{:S(2)}) %collective-permute-start.3) | collective-permute-done | bytes 57376 | tf_op jit(solution)/shard_map/ppermute | solution.py:17
  12.7 0.0 copy-done
  12.7 0.0 copy-done.1
  12.7 0.0 copy-done.2
  12.7 0.1 shard_map.87.refs_0_
  12.8 0.1 collective-permute-start.5
  12.9 0.9 %collective-permute-start.6 = (bf16[112,128]{1,0:T(8,128)(2,1)S(1)}, bf16[112,128]{1,0:T(8,128)(2,1)S(1)}, u32[]{:S(2)}, u32[]{:S(2)}) collective-permute-start(bf16[112,128]{1,0:T(8,128)(2,1)S(1)} %shard_map.87.refs_0_), channel_id=1, source_target_pairs={{0,2},{1,3},{2,0},{3,1},{16,18},{17,19},{18,16},{19,17},{4,6},{5,7... | collective-permute-start | bytes 86024 | tf_op jit(solution)/shard_map/ppermute | solution.py:17
  13.8 0.9 %collective-permute-start.7 = (bf16[112,128]{1,0:T(8,128)(2,1)S(1)}, bf16[112,128]{1,0:T(8,128)(2,1)S(1)}, u32[]{:S(2)}, u32[]{:S(2)}) collective-permute-start(bf16[112,128]{1,0:T(8,128)(2,1)S(1)} %shard_map.87.refs_0_), channel_id=1, source_target_pairs={{0,3},{1,2},{2,1},{3,0},{16,19},{17,18},{18,17},{19,16},{4,7},{5,6... | collective-permute-start | bytes 86024 | tf_op jit(solution)/shard_map/ppermute | solution.py:17
  14.7 0.7 %shard_map.86 = (f32[56,128]{1,0:T(8,128)}, f32[56,128]{1,0:T(8,128)}, f32[56,128]{1,0:T(8,128)}) custom-call(s32[1]{0:T(128)S(6)} %copy.9.step_ref, f32[112,128]{1,0:T(8,128)S(1)} %get-tuple-element.13.keep, f32[112,128]{1,0:T(8,128)S(1)} %collective-permute-done.1.near, f32[112,128]{1,0:T(8,128)S(1)} %collective-permute-done.2.level, ...), custom_call_target="tpu_custom_call" | custom-call | tf_op jit(solution)/shard_map/pallas_call | solution.py:90
  15.4 0.0 collective-permute-done.5.refs_1_
  15.4 1.4 %collective-permute-done.6.refs_2_ = bf16[112,128]{1,0:T(8,128)(2,1)S(1)} collective-permute-done((bf16[112,128]{1,0:T(8,128)(2,1)S(1)}, bf16[112,128]{1,0:T(8,128)(2,1)S(1)}, u32[]{:S(2)}, u32[]{:S(2)}) %collective-permute-start.6) | collective-permute-done | bytes 28704 | tf_op jit(solution)/shard_map/ppermute | solution.py:17
  16.8 0.3 %collective-permute-done.7.refs_3_ = bf16[112,128]{1,0:T(8,128)(2,1)S(1)} collective-permute-done((bf16[112,128]{1,0:T(8,128)(2,1)S(1)}, bf16[112,128]{1,0:T(8,128)(2,1)S(1)}, u32[]{:S(2)}, u32[]{:S(2)}) %collective-permute-start.7) | collective-permute-done | bytes 28704 | tf_op jit(solution)/shard_map/ppermute | solution.py:17
  17.1 0.7 %shard_map.88 = bf16[448,128]{1,0:T(8,128)(2,1)} custom-call(bf16[112,128]{1,0:T(8,128)(2,1)S(1)} %shard_map.87.refs_0_, bf16[112,128]{1,0:T(8,128)(2,1)S(1)} %collective-permute-done.5.refs_1_, bf16[112,128]{1,0:T(8,128)(2,1)S(1)} %collective-permute-done.6.refs_2_, bf16[112,128]{1,0:T(8,128)(2,1)S(1)} %collective-permute-done.7.refs_3_), custom_call_target="tpu_custom_call" | custom-call | tf_op jit(solution)/shard_map/pallas_call | solution.py:90
  (1 shorter events, 0.0 us)
Async XLA Ops:
  0.6 4.8 %collective-permute-start = (f32[448,128]{1,0:T(8,128)}, f32[448,128]{1,0:T(8,128)S(1)}, u32[]{:S(2)}, u32[]{:S(2)}) collective-permute-start(f32[448,128]{1,0:T(8,128)} %bitcast.25), channel_id=1, source_target_pairs={{0,1},{1,0},{2,3},{3,2},{16,17},{17,16},{18,19},{19,18},{4,5},{5,4... | collective-permute-start | bytes 688136 | tf_op jit(solution)/shard_map/ppermute | solution.py:17
  1.9 7.8 %collective-permute-start.4 = (f32[168,128]{1,0:T(8,128)S(1)}, f32[168,128]{1,0:T(8,128)S(1)}, u32[]{:S(2)}, u32[]{:S(2)}) collective-permute-start(f32[168,128]{1,0:T(8,128)S(1)} %pad_maximum_fusion), channel_id=1, source_target_pairs={{0,16},{1,17},{2,18},{3,19},{16,0},{17,1},{18,2},{19,3},{4,20},{5,... | collective-permute-start | bytes 258056 | tf_op jit(solution)/shard_map/ppermute | solution.py:17
  4.5 0.9 %copy-start.3 = (f32[1,1,8,7168]{3,2,1,0:T(8,128)S(1)}, f32[1,1,8,7168]{3,2,1,0:T(8,128)}, u32[]{:S(2)}) copy-start(f32[1,1,8,7168]{3,2,1,0:T(8,128)} %param.5) | copy-start | bytes 688132
  5.5 7.2 %copy-start = (f32[1,7168]{1,0:T(1,128)S(1)}, f32[1,7168]{1,0:T(1,128)}, u32[]{:S(2)}) copy-start(f32[1,7168]{1,0:T(1,128)} %param.6) | copy-start | bytes 86020
  5.5 7.2 %copy-start.1 = (f32[1,7168]{1,0:T(1,128)S(1)}, f32[1,7168]{1,0:T(1,128)}, u32[]{:S(2)}) copy-start(f32[1,7168]{1,0:T(1,128)} %param.7) | copy-start | bytes 86020
  5.5 7.2 %copy-start.2 = (f32[1,7168]{1,0:T(1,128)S(1)}, f32[1,7168]{1,0:T(1,128)}, u32[]{:S(2)}) copy-start(f32[1,7168]{1,0:T(1,128)} %param.8) | copy-start | bytes 86020
  5.5 4.2 %collective-permute-start.2 = (f32[112,128]{1,0:T(8,128)S(1)}, f32[112,128]{1,0:T(8,128)S(1)}, u32[]{:S(2)}, u32[]{:S(2)}) collective-permute-start(f32[112,128]{1,0:T(8,128)S(1)} %get-tuple-element.13.keep), channel_id=1, source_target_pairs={{0,16},{1,17},{2,18},{3,19},{16,0},{17,1},{18,2},{19,3},{4,20},{5,... | collective-permute-start | bytes 172040 | tf_op jit(solution)/shard_map/ppermute | solution.py:17
  5.6 4.2 %collective-permute-start.1 = (f32[112,128]{1,0:T(8,128)S(1)}, f32[112,128]{1,0:T(8,128)S(1)}, u32[]{:S(2)}, u32[]{:S(2)}) collective-permute-start(f32[112,128]{1,0:T(8,128)S(1)} %get-tuple-element.14), channel_id=1, source_target_pairs={{0,2},{1,3},{2,0},{3,1},{16,18},{17,19},{18,16},{19,17},{4,6},{5,7... | collective-permute-start | bytes 172040 | tf_op jit(solution)/shard_map/ppermute | solution.py:17
  7.6 5.1 %collective-permute-start.3 = (f32[112,128]{1,0:T(8,128)S(1)}, f32[112,128]{1,0:T(8,128)S(1)}, u32[]{:S(2)}, u32[]{:S(2)}) collective-permute-start(f32[112,128]{1,0:T(8,128)S(1)} %get-tuple-element.14), channel_id=1, source_target_pairs={{0,18},{1,19},{2,16},{3,17},{16,2},{17,3},{18,0},{19,1},{4,22},{5,... | collective-permute-start | bytes 172040 | tf_op jit(solution)/shard_map/ppermute | solution.py:17
  12.8 2.6 %collective-permute-start.5 = (bf16[112,128]{1,0:T(8,128)(2,1)S(1)}, bf16[112,128]{1,0:T(8,128)(2,1)S(1)}, u32[]{:S(2)}, u32[]{:S(2)}) collective-permute-start(bf16[112,128]{1,0:T(8,128)(2,1)S(1)} %shard_map.87.refs_0_), channel_id=1, source_target_pairs={{0,1},{1,0},{2,3},{3,2},{16,17},{17,16},{18,19},{19,18},{4,5},{5,4... | collective-permute-start | bytes 86024 | tf_op jit(solution)/shard_map/ppermute | solution.py:17
  12.9 4.0 %collective-permute-start.6 = (bf16[112,128]{1,0:T(8,128)(2,1)S(1)}, bf16[112,128]{1,0:T(8,128)(2,1)S(1)}, u32[]{:S(2)}, u32[]{:S(2)}) collective-permute-start(bf16[112,128]{1,0:T(8,128)(2,1)S(1)} %shard_map.87.refs_0_), channel_id=1, source_target_pairs={{0,2},{1,3},{2,0},{3,1},{16,18},{17,19},{18,16},{19,17},{4,6},{5,7... | collective-permute-start | bytes 86024 | tf_op jit(solution)/shard_map/ppermute | solution.py:17
  13.8 3.3 %collective-permute-start.7 = (bf16[112,128]{1,0:T(8,128)(2,1)S(1)}, bf16[112,128]{1,0:T(8,128)(2,1)S(1)}, u32[]{:S(2)}, u32[]{:S(2)}) collective-permute-start(bf16[112,128]{1,0:T(8,128)(2,1)S(1)} %shard_map.87.refs_0_), channel_id=1, source_target_pairs={{0,3},{1,2},{2,1},{3,0},{16,19},{17,18},{18,17},{19,16},{4,7},{5,6... | collective-permute-start | bytes 86024 | tf_op jit(solution)/shard_map/ppermute | solution.py:17
where the time goes:
time: 18.1 us; the launch traced here: 17.8 us
  starting transfers between devices  8.53 us (47%)
  waiting for transfers between devices  4.65 us (26%)
  Pallas kernels  1.55 us (9%)
  between operations  1.35 us (7%)
  local copies, waits for them, and re-layouts  0.96 us (5%)
  other arithmetic  0.79 us (4%)
    ppermute x8, starting transfers between devices, swap(): return lax.ppermute(array, GROUP, [(i, i ^ bit) for i in range(size)])  8.53 us
    ppermute x8, waiting for transfers between devices, swap(): return lax.ppermute(array, GROUP, [(i, i ^ bit) for i in range(size)])  4.65 us
    pallas_call x5, Pallas kernels, call(): pl.pallas_call(body, out_shape=outs, in_specs=specs, out_specs=jax.tree.m...  1.55 us
    unnamed x8, local copies, waits for them, and re-layouts  0.96 us
    concatenate x1, other arithmetic, per_device(): state = swap(jnp.concatenate([master, moment, second], axis=0), shards)  0.79 us
  transfers between devices with their start and end apart: 8, of which 4 were waited for; matrix products, arithmetic and copies ran while one was open for 4% of the time, Pallas kernels for 4%

commit v1 on v0

--- a/solution.py
+++ b/solution.py
@@ -22,21 +22,38 @@
     return pl.ds((row // sub) * (tiles * sub) + row % sub, tiles, stride=sub)
 
 
-def pick_kernel(pairs, shards, own, tiles, *refs):
-    source_ref, added, (keep_ref, give_ref) = refs[0], refs[1:-2], refs[-2:]
+def my_rows(pairs, shards, own, tiles):
     shard = lax.axis_index("dp")
     core, near = shard & 1, shard & 2
-    rows = pairs * shards * own
-    slot = 0
+    rows, slot = pairs * shards * own, 0
     for pair in range(pairs):
         for far in range(shards // 4):
             for o in range(own):
-                to = slice(slot * tiles, (slot + 1) * tiles)
-                for i, (out_ref, bit) in enumerate(((keep_ref, near), (give_ref, 2 - near))):
-                    row = (pair * shards + far * 4 + bit + core) * own + o
-                    picked = source_ref[row_at(row, tiles, rows), :]
-                    out_ref[to, :] = picked + added[i][to, :] if added else picked
+                first = pair * shards + far * 4 + core
+                at = [row_at((first + bit) * own + o, tiles, rows) for bit in (near, 2 - near)]
+                yield slice(slot * tiles, (slot + 1) * tiles), at
                 slot += 1
+
+
+def front_kernel(dims, local, master, moment, second, keep_ref, give_ref, state_ref, held, sems):
+    size = master.shape[0]
+    copies = [pltpu.make_async_copy(local, held, sems.at[3])]
+    for i, source in enumerate((master, moment, second)):
+        to = state_ref.at[pl.ds(i * size, size), :]
+        copies.append(pltpu.make_async_copy(source, to, sems.at[i]))
+    for copy in copies:
+        copy.start()
+    for copy in copies:
+        copy.wait()
+    for to, (mine, other) in my_rows(*dims):
+        keep_ref[to, :] = held[mine, :]
+        give_ref[to, :] = held[other, :]
+
+
+def sum_kernel(dims, theirs, own_keep, own_give, give_ref, keep_ref):
+    for to, (mine, other) in my_rows(*dims):
+        keep_ref[to, :] = own_keep[to, :] + theirs[mine, :]
+        give_ref[to, :] = own_give[to, :] + theirs[other, :]
 
 
 def adam(total, master, moment, second, count):
@@ -49,29 +66,33 @@
 
 
 def totals(size, sums):
-    keep, near, level, cross = (s[...] for s in sums)
+    cross, near, level, keep = (s[...] for s in sums)
     both = (keep + near) + (level + cross)
     first = lax.axis_index("pair") == 0
     low, high = both[:size], both[size:]
     return jnp.where(first, low, high), jnp.where(first, high, low)
 
 
-def params_kernel(size, step_ref, keep, near, level, cross, master, moment, second, state, out_ref):
+def thirds(size, ref):
+    return [ref[i * size:(i + 1) * size, :] for i in range(3)]
+
+
+def params_kernel(size, step_ref, cross, near, level, keep, state, theirs_state, out_ref):
     count = jnp.full((1, LANES), step_ref[0], jnp.int32).astype(jnp.float32)
-    mine, theirs = totals(size, (keep, near, level, cross))
-    a, _, _ = adam(mine, master[...], moment[...], second[...], count)
-    b, _, _ = adam(theirs, state[:size], state[size:2 * size], state[2 * size:], count)
+    mine, theirs = totals(size, (cross, near, level, keep))
+    a, _, _ = adam(mine, *thirds(size, state), count)
+    b, _, _ = adam(theirs, *thirds(size, theirs_state), count)
     out_ref[...] = jnp.concatenate([a, b], axis=0).astype(out_ref.dtype)
 
 
-def own_kernel(size, step_ref, keep, near, level, cross, master, moment, second, m_ref, v_ref, s_ref):
+def own_kernel(size, step_ref, cross, near, level, keep, state, m_ref, v_ref, s_ref):
     count = jnp.full((1, LANES), step_ref[0], jnp.int32).astype(jnp.float32)
-    mine, _ = totals(size, (keep, near, level, cross))
-    m_ref[...], v_ref[...], s_ref[...] = adam(mine, master[...], moment[...], second[...], count)
+    mine, _ = totals(size, (cross, near, level, keep))
+    m_ref[...], v_ref[...], s_ref[...] = adam(mine, *thirds(size, state), count)
 
 
 def order_kernel(pairs, shards, own, tiles, *refs):
-    pieces, out_ref, scratch = refs[:4], refs[4], refs[5]
+    pieces, out_ref, scratch = refs[3::-1], refs[4], refs[5]
     pair, shard = lax.axis_index("pair"), lax.axis_index("dp") & 3
     rows = pairs * 4 * own
     for k in range(4):
@@ -84,9 +105,10 @@
     out_ref[...] = scratch[...].astype(out_ref.dtype)
 
 
-def call(body, outs, *args, scratch=()):
+def call(body, outs, *args, hbm=False, scratch=()):
+    space = pltpu.HBM if hbm else pltpu.VMEM
+    specs = [pl.BlockSpec(memory_space=pltpu.SMEM if a.dtype == jnp.int32 else space) for a in args]
     held = sum(math.prod(a.shape) * a.dtype.itemsize for a in [*args, *jax.tree.leaves(outs)])
-    specs = [pl.BlockSpec(memory_space=pltpu.SMEM if a.dtype == jnp.int32 else pltpu.VMEM) for a in args]
     return pl.pallas_call(
         body,
         out_shape=outs,
@@ -110,12 +132,15 @@
     sub = min(8, rows)
     local = grads.reshape(rows // sub, sub, tiles, LANES).transpose(0, 2, 1, 3).reshape(rows * tiles, LANES)
 
+    dims = (pairs, shards, own, tiles)
     theirs = swap(local, 1)
-    state = swap(jnp.concatenate([master, moment, second], axis=0), shards)
     half = shaped((pairs * (shards // 4) * size, LANES), f32)
-    pick = functools.partial(pick_kernel, pairs, shards, own, tiles)
-    mine = call(pick, (half, half), local)
-    keep, give = call(pick, (half, half), theirs, *mine)
+    keep, give, state = call(
+        functools.partial(front_kernel, dims), (half, half, shaped((3 * size, LANES), f32)),
+        *(pltpu.with_memory_space_constraint(a, pltpu.HBM) for a in (local, master, moment, second)), hbm=True,
+        scratch=[pltpu.VMEM(local.shape, f32), pltpu.SemaphoreType.DMA((4,))])
+    theirs_state = swap(state, shards)
+    give, keep = call(functools.partial(sum_kernel, dims), (half, half), theirs, keep, give)
 
     for bit in reversed(far):
         low = (shard & bit) == 0
@@ -124,18 +149,17 @@
         other = jnp.where(low, held[:, :, 1], held[:, :, 0])
         keep, give = (mine + swap(other, bit)).reshape(2, -1, LANES)
 
-    near, cross = swap(give, 2), swap(give, shards | 2)
-    level = swap(keep, shards)
-    sums = (keep, near, level, cross)
+    cross, near, level = swap(give, shards | 2), swap(give, 2), swap(keep, shards)
+    sums = (cross, near, level, keep)
 
     params = call(
         functools.partial(params_kernel, size), shaped((pairs * size, LANES), jnp.bfloat16),
-        step, *sums, master, moment, second, state)
+        step, *sums, state, theirs_state)
     row = shaped((size, LANES), f32)
     news = call(
-        functools.partial(own_kernel, size), (row, row, row), step, *sums, master, moment, second)
+        functools.partial(own_kernel, size), (row, row, row), step, *sums, state)
 
-    pieces = [params, swap(params, 1), swap(params, 2), swap(params, 3)]
+    pieces = [swap(params, bit) for bit in (3, 2, 1)] + [params]
     block = pairs * 4 * size
     params = call(
         functools.partial(order_kernel, pairs, shards, own, tiles), shaped((block, LANES), jnp.bfloat16),

time: 18.1 us -> 17.2 us (0.950)
  Pallas kernels: 1.55 us -> 2.52 us
  local copies, waits for them, and re-layouts: 0.96 us -> 0 us
  other arithmetic: 0.79 us -> 0 us
    pallas_call x5, Pallas kernels: 1.55 us -> 2.52 us  [call(): pl.pallas_call(body, out_shape=outs, in_specs=specs, out_specs=jax.tree.m...]
    unnamed x8 -> x0, local copies, waits for them, and re-layouts: 0.96 us -> none
    concatenate x1 -> x0, other arithmetic: 0.79 us -> none  [per_device(): state = swap(jnp.concatenate([master, moment, second], axis=0), shards)]
  transfers between devices with their start and end apart: 8 -> 8, of which waited for: 4 -> 5; matrix products, arithmetic and copies ran while one was open for 4% -> 0% of each run, Pallas kernels for 4% -> 10%
where the time goes in v1:
time: 17.2 us; the launch traced here: 17 us
  starting transfers between devices  8.59 us (50%)
  waiting for transfers between devices  4.59 us (27%)
  Pallas kernels  2.52 us (15%)
  between operations  1.32 us (8%)
    ppermute x8, starting transfers between devices, swap(): return lax.ppermute(array, GROUP, [(i, i ^ bit) for i in range(size)])  8.59 us
    ppermute x8, waiting for transfers between devices, swap(): return lax.ppermute(array, GROUP, [(i, i ^ bit) for i in range(size)])  4.59 us
    pallas_call x5, Pallas kernels, call(): pl.pallas_call(body, out_shape=outs, in_specs=specs, out_specs=jax.tree.m...  2.52 us
  transfers between devices with their start and end apart: 8, of which 5 were waited for; matrix products, arithmetic and copies ran while one was open for 0% of the time, Pallas kernels for 10%

profile of v1, /device:TPU:0, one launch (start us, length us, event | category | flops | bytes accessed | tf_op | source)
XLA Modules:
  0.0 17.0 jit_solution(10027693729241765659)
XLA Ops:
  0.6 0.5 %collective-permute-start = (f32[448,128]{1,0:T(8,128)}, f32[448,128]{1,0:T(8,128)S(1)}, u32[]{:S(2)}, u32[]{:S(2)}) collective-permute-start(f32[448,128]{1,0:T(8,128)} %bitcast.16), channel_id=1, source_target_pairs={{0,1},{1,0},{2,3},{3,2},{16,17},{17,16},{18,19},{19,18},{4,5},{5,4... | collective-permute-start | bytes 688136 | tf_op jit(solution)/shard_map/ppermute | solution.py:17
  1.1 1.0 %shard_map.84 = (f32[112,128]{1,0:T(8,128)S(1)}, f32[112,128]{1,0:T(8,128)S(1)}, f32[168,128]{1,0:T(8,128)S(1)}) custom-call(f32[448,128]{1,0:T(8,128)} %bitcast.17, f32[56,128]{1,0:T(8,128)} %bitcast.19, f32[56,128]{1,0:T(8,128)} %bitcast.20, f32[56,128]{1,0:T(8,128)} %bitcast.21), custom_call_target="tpu_custom_call" | custom-call | tf_op jit(solution)/shard_map/pallas_call | solution.py:112
  2.2 2.6 %collective-permute-start.4 = (f32[168,128]{1,0:T(8,128)S(1)}, f32[168,128]{1,0:T(8,128)S(1)}, u32[]{:S(2)}, u32[]{:S(2)}) collective-permute-start(f32[168,128]{1,0:T(8,128)S(1)} %get-tuple-element.16.state), channel_id=1, source_target_pairs={{0,16},{1,17},{2,18},{3,19},{16,0},{17,1},{18,2},{19,3},{4,20},{5,... | collective-permute-start | bytes 258056 | tf_op jit(solution)/shard_map/ppermute | solution.py:17
  4.8 0.0 collective-permute-done.theirs
  4.8 0.7 %collective-permute-start.3 = (f32[112,128]{1,0:T(8,128)S(1)}, f32[112,128]{1,0:T(8,128)S(1)}, u32[]{:S(2)}, u32[]{:S(2)}) collective-permute-start(f32[112,128]{1,0:T(8,128)S(1)} %get-tuple-element.15.keep), channel_id=1, source_target_pairs={{0,16},{1,17},{2,18},{3,19},{16,0},{17,1},{18,2},{19,3},{4,20},{5,... | collective-permute-start | bytes 172040 | tf_op jit(solution)/shard_map/ppermute | solution.py:17
  5.5 2.4 %collective-permute-start.1 = (f32[112,128]{1,0:T(8,128)S(1)}, f32[112,128]{1,0:T(8,128)S(1)}, u32[]{:S(2)}, u32[]{:S(2)}) collective-permute-start(f32[112,128]{1,0:T(8,128)S(1)} %get-tuple-element.14), channel_id=1, source_target_pairs={{0,18},{1,19},{2,16},{3,17},{16,2},{17,3},{18,0},{19,1},{4,22},{5,... | collective-permute-start | bytes 172040 | tf_op jit(solution)/shard_map/ppermute | solution.py:17
  7.8 0.5 %collective-permute-start.2 = (f32[112,128]{1,0:T(8,128)S(1)}, f32[112,128]{1,0:T(8,128)S(1)}, u32[]{:S(2)}, u32[]{:S(2)}) collective-permute-start(f32[112,128]{1,0:T(8,128)S(1)} %get-tuple-element.14), channel_id=1, source_target_pairs={{0,2},{1,3},{2,0},{3,1},{16,18},{17,19},{18,16},{19,17},{4,6},{5,7... | collective-permute-start | bytes 172040 | tf_op jit(solution)/shard_map/ppermute | solution.py:17
  9.0 0.0 collective-permute-done.4.theirs_state
  9.0 0.8 %collective-permute-done.3.level = f32[112,128]{1,0:T(8,128)S(1)} collective-permute-done((f32[112,128]{1,0:T(8,128)S(1)}, f32[112,128]{1,0:T(8,128)S(1)}, u32[]{:S(2)}, u32[]{:S(2)}) %collective-permute-start.3) | collective-permute-done | bytes 57376 | tf_op jit(solution)/shard_map/ppermute | solution.py:17
  9.8 1.3 %collective-permute-done.1.cross = f32[112,128]{1,0:T(8,128)S(1)} collective-permute-done((f32[112,128]{1,0:T(8,128)S(1)}, f32[112,128]{1,0:T(8,128)S(1)}, u32[]{:S(2)}, u32[]{:S(2)}) %collective-permute-start.1) | collective-permute-done | bytes 57376 | tf_op jit(solution)/shard_map/ppermute | solution.py:17
  11.1 0.9 %collective-permute-done.2.near = f32[112,128]{1,0:T(8,128)S(1)} collective-permute-done((f32[112,128]{1,0:T(8,128)S(1)}, f32[112,128]{1,0:T(8,128)S(1)}, u32[]{:S(2)}, u32[]{:S(2)}) %collective-permute-start.2) | collective-permute-done | bytes 57376 | tf_op jit(solution)/shard_map/ppermute | solution.py:17
  12.0 0.1 shard_map.87.refs_3_
  12.1 0.1 collective-permute-start.5
  12.2 0.9 %collective-permute-start.6 = (bf16[112,128]{1,0:T(8,128)(2,1)S(1)}, bf16[112,128]{1,0:T(8,128)(2,1)S(1)}, u32[]{:S(2)}, u32[]{:S(2)}) collective-permute-start(bf16[112,128]{1,0:T(8,128)(2,1)S(1)} %shard_map.87.refs_3_), channel_id=1, source_target_pairs={{0,2},{1,3},{2,0},{3,1},{16,18},{17,19},{18,16},{19,17},{4,6},{5,7... | collective-permute-start | bytes 86024 | tf_op jit(solution)/shard_map/ppermute | solution.py:17
  13.0 1.0 %collective-permute-start.7 = (bf16[112,128]{1,0:T(8,128)(2,1)S(1)}, bf16[112,128]{1,0:T(8,128)(2,1)S(1)}, u32[]{:S(2)}, u32[]{:S(2)}) collective-permute-start(bf16[112,128]{1,0:T(8,128)(2,1)S(1)} %shard_map.87.refs_3_), channel_id=1, source_target_pairs={{0,1},{1,0},{2,3},{3,2},{16,17},{17,16},{18,19},{19,18},{4,5},{5,4... | collective-permute-start | bytes 86024 | tf_op jit(solution)/shard_map/ppermute | solution.py:17
  14.0 0.7 %shard_map.86 = (f32[56,128]{1,0:T(8,128)}, f32[56,128]{1,0:T(8,128)}, f32[56,128]{1,0:T(8,128)}) custom-call(s32[1]{0:T(128)S(6)} %copy.9.step_ref, f32[112,128]{1,0:T(8,128)S(1)} %collective-permute-done.1.cross, f32[112,128]{1,0:T(8,128)S(1)} %collective-permute-done.2.near, f32[112,128]{1,0:T(8,128)S(1)} %collective-permute-done.3.level, ...), custom_call_target="tpu_custom_call" | custom-call | tf_op jit(solution)/shard_map/pallas_call | solution.py:112
  14.7 0.8 %collective-permute-done.5.refs_0_ = bf16[112,128]{1,0:T(8,128)(2,1)S(1)} collective-permute-done((bf16[112,128]{1,0:T(8,128)(2,1)S(1)}, bf16[112,128]{1,0:T(8,128)(2,1)S(1)}, u32[]{:S(2)}, u32[]{:S(2)}) %collective-permute-start.5) | collective-permute-done | bytes 28704 | tf_op jit(solution)/shard_map/ppermute | solution.py:17
  15.4 0.8 %collective-permute-done.6.refs_1_ = bf16[112,128]{1,0:T(8,128)(2,1)S(1)} collective-permute-done((bf16[112,128]{1,0:T(8,128)(2,1)S(1)}, bf16[112,128]{1,0:T(8,128)(2,1)S(1)}, u32[]{:S(2)}, u32[]{:S(2)}) %collective-permute-start.6) | collective-permute-done | bytes 28704 | tf_op jit(solution)/shard_map/ppermute | solution.py:17
  16.3 0.0 collective-permute-done.7.refs_2_
  16.3 0.7 %shard_map.88 = bf16[448,128]{1,0:T(8,128)(2,1)} custom-call(bf16[112,128]{1,0:T(8,128)(2,1)S(1)} %collective-permute-done.5.refs_0_, bf16[112,128]{1,0:T(8,128)(2,1)S(1)} %collective-permute-done.6.refs_1_, bf16[112,128]{1,0:T(8,128)(2,1)S(1)} %collective-permute-done.7.refs_2_, bf16[112,128]{1,0:T(8,128)(2,1)S(1)} %shard_map.87.refs_3_), custom_call_target="tpu_custom_call" | custom-call | tf_op jit(solution)/shard_map/pallas_call | solution.py:112
  (1 shorter events, 0.0 us)
Async XLA Ops:
  0.6 4.1 %collective-permute-start = (f32[448,128]{1,0:T(8,128)}, f32[448,128]{1,0:T(8,128)S(1)}, u32[]{:S(2)}, u32[]{:S(2)}) collective-permute-start(f32[448,128]{1,0:T(8,128)} %bitcast.16), channel_id=1, source_target_pairs={{0,1},{1,0},{2,3},{3,2},{16,17},{17,16},{18,19},{19,18},{4,5},{5,4... | collective-permute-start | bytes 688136 | tf_op jit(solution)/shard_map/ppermute | solution.py:17
  2.2 6.8 %collective-permute-start.4 = (f32[168,128]{1,0:T(8,128)S(1)}, f32[168,128]{1,0:T(8,128)S(1)}, u32[]{:S(2)}, u32[]{:S(2)}) collective-permute-start(f32[168,128]{1,0:T(8,128)S(1)} %get-tuple-element.16.state), channel_id=1, source_target_pairs={{0,16},{1,17},{2,18},{3,19},{16,0},{17,1},{18,2},{19,3},{4,20},{5,... | collective-permute-start | bytes 258056 | tf_op jit(solution)/shard_map/ppermute | solution.py:17
  4.8 5.0 %collective-permute-start.3 = (f32[112,128]{1,0:T(8,128)S(1)}, f32[112,128]{1,0:T(8,128)S(1)}, u32[]{:S(2)}, u32[]{:S(2)}) collective-permute-start(f32[112,128]{1,0:T(8,128)S(1)} %get-tuple-element.15.keep), channel_id=1, source_target_pairs={{0,16},{1,17},{2,18},{3,19},{16,0},{17,1},{18,2},{19,3},{4,20},{5,... | collective-permute-start | bytes 172040 | tf_op jit(solution)/shard_map/ppermute | solution.py:17
  5.5 5.6 %collective-permute-start.1 = (f32[112,128]{1,0:T(8,128)S(1)}, f32[112,128]{1,0:T(8,128)S(1)}, u32[]{:S(2)}, u32[]{:S(2)}) collective-permute-start(f32[112,128]{1,0:T(8,128)S(1)} %get-tuple-element.14), channel_id=1, source_target_pairs={{0,18},{1,19},{2,16},{3,17},{16,2},{17,3},{18,0},{19,1},{4,22},{5,... | collective-permute-start | bytes 172040 | tf_op jit(solution)/shard_map/ppermute | solution.py:17
  7.8 4.2 %collective-permute-start.2 = (f32[112,128]{1,0:T(8,128)S(1)}, f32[112,128]{1,0:T(8,128)S(1)}, u32[]{:S(2)}, u32[]{:S(2)}) collective-permute-start(f32[112,128]{1,0:T(8,128)S(1)} %get-tuple-element.14), channel_id=1, source_target_pairs={{0,2},{1,3},{2,0},{3,1},{16,18},{17,19},{18,16},{19,17},{4,6},{5,7... | collective-permute-start | bytes 172040 | tf_op jit(solution)/shard_map/ppermute | solution.py:17
  12.1 3.4 %collective-permute-start.5 = (bf16[112,128]{1,0:T(8,128)(2,1)S(1)}, bf16[112,128]{1,0:T(8,128)(2,1)S(1)}, u32[]{:S(2)}, u32[]{:S(2)}) collective-permute-start(bf16[112,128]{1,0:T(8,128)(2,1)S(1)} %shard_map.87.refs_3_), channel_id=1, source_target_pairs={{0,3},{1,2},{2,1},{3,0},{16,19},{17,18},{18,17},{19,16},{4,7},{5,6... | collective-permute-start | bytes 86024 | tf_op jit(solution)/shard_map/ppermute | solution.py:17
  12.2 4.1 %collective-permute-start.6 = (bf16[112,128]{1,0:T(8,128)(2,1)S(1)}, bf16[112,128]{1,0:T(8,128)(2,1)S(1)}, u32[]{:S(2)}, u32[]{:S(2)}) collective-permute-start(bf16[112,128]{1,0:T(8,128)(2,1)S(1)} %shard_map.87.refs_3_), channel_id=1, source_target_pairs={{0,2},{1,3},{2,0},{3,1},{16,18},{17,19},{18,16},{19,17},{4,6},{5,7... | collective-permute-start | bytes 86024 | tf_op jit(solution)/shard_map/ppermute | solution.py:17
  13.0 3.2 %collective-permute-start.7 = (bf16[112,128]{1,0:T(8,128)(2,1)S(1)}, bf16[112,128]{1,0:T(8,128)(2,1)S(1)}, u32[]{:S(2)}, u32[]{:S(2)}) collective-permute-start(bf16[112,128]{1,0:T(8,128)(2,1)S(1)} %shard_map.87.refs_3_), channel_id=1, source_target_pairs={{0,1},{1,0},{2,3},{3,2},{16,17},{17,16},{18,19},{19,18},{4,5},{5,4... | collective-permute-start | bytes 86024 | tf_op jit(solution)/shard_map/ppermute | solution.py:17

commit v2 on v1

--- a/solution.py
+++ b/solution.py
@@ -12,9 +12,10 @@
 LANES = 128
 
 
-def swap(array, bit):
+def send(array, bits, core_1_bits=None):
     size = lax.axis_size(GROUP)
-    return lax.ppermute(array, GROUP, [(i, i ^ bit) for i in range(size)])
+    flip = (bits, bits if core_1_bits is None else core_1_bits)
+    return lax.ppermute(array, GROUP, [(i, i ^ flip[i & 1]) for i in range(size)])
 
 
 def row_at(row, tiles, rows):
@@ -22,17 +23,25 @@
     return pl.ds((row // sub) * (tiles * sub) + row % sub, tiles, stride=sub)
 
 
-def my_rows(pairs, shards, own, tiles):
-    shard = lax.axis_index("dp")
-    core, near = shard & 1, shard & 2
-    rows, slot = pairs * shards * own, 0
-    for pair in range(pairs):
+def place(slot, other):
+    pair, shard = lax.axis_index("pair"), lax.axis_index("dp")
+    core, near = shard & 1, (shard >> 1) & 1
+    return pair ^ (slot * (1 - core)) ^ (other * core), near ^ (slot * core) ^ (other * (1 - core))
+
+
+def my_rows(shards, own, tiles):
+    core = lax.axis_index("dp") & 1
+    rows, i = 2 * shards * own, 0
+    for slot in range(2):
+        kept, given = place(slot, 0), place(slot, 1)
         for far in range(shards // 4):
             for o in range(own):
-                first = pair * shards + far * 4 + core
-                at = [row_at((first + bit) * own + o, tiles, rows) for bit in (near, 2 - near)]
-                yield slice(slot * tiles, (slot + 1) * tiles), at
-                slot += 1
+                at = [
+                    row_at((pair * shards + far * 4 + near * 2 + core) * own + o, tiles, rows)
+                    for pair, near in (kept, given)
+                ]
+                yield slice(i * tiles, (i + 1) * tiles), at
+                i += 1
 
 
 def front_kernel(dims, local, master, moment, second, keep_ref, give_ref, state_ref, held, sems):
@@ -67,10 +76,11 @@
 
 def totals(size, sums):
     cross, near, level, keep = (s[...] for s in sums)
-    both = (keep + near) + (level + cross)
-    first = lax.axis_index("pair") == 0
-    low, high = both[:size], both[size:]
-    return jnp.where(first, low, high), jnp.where(first, high, low)
+    flip = lambda rows: (rows[size:], rows[:size])
+    return [
+        (c + n) + (l + k)
+        for c, n, l, k in zip(flip(cross), flip(near)[::-1], flip(level), flip(keep)[::-1])
+    ]
 
 
 def thirds(size, ref):
@@ -91,17 +101,23 @@
     m_ref[...], v_ref[...], s_ref[...] = adam(mine, *thirds(size, state), count)
 
 
-def order_kernel(pairs, shards, own, tiles, *refs):
-    pieces, out_ref, scratch = refs[3::-1], refs[4], refs[5]
-    pair, shard = lax.axis_index("pair"), lax.axis_index("dp") & 3
-    rows = pairs * 4 * own
-    for k in range(4):
-        piece = pieces[k][...].astype(jnp.float32)
-        for s in range(pairs):
+def order_kernel(own, tiles, *refs):
+    pieces, out_ref, scratch = refs[:4], refs[4], refs[5]
+    pair, shard = lax.axis_index("pair"), lax.axis_index("dp")
+    core, near = shard & 1, (shard >> 1) & 1
+    sources = (
+        (pair ^ (1 - core), near ^ core, core ^ 1),
+        (pair ^ core, near ^ (1 - core), core),
+        (pair, near, core ^ 1),
+        (pair, near, core),
+    )
+    for ref, (p, n, c) in zip(pieces, sources):
+        piece = ref[...].astype(jnp.float32)
+        for slot in range(2):
             for o in range(own):
-                row = ((pair ^ s) * 4 + (shard ^ k)) * own + o
-                start = (s * own + o) * tiles
-                scratch[row_at(row, tiles, rows), :] = piece[start:start + tiles]
+                row = ((p ^ (slot * (1 - c))) * 4 + (n ^ (slot * c)) * 2 + c) * own + o
+                start = (slot * own + o) * tiles
+                scratch[row_at(row, tiles, 8 * own), :] = piece[start:start + tiles]
     out_ref[...] = scratch[...].astype(out_ref.dtype)
 
 
@@ -122,7 +138,7 @@
 def per_device(grads, master, moment, second, step):
     rows, width = grads.shape[2], grads.shape[3]
     own, tiles = master.shape[0], width // LANES
-    pairs, shards = lax.axis_size("pair"), lax.axis_size("dp")
+    shards = lax.axis_size("dp")
     shard = lax.axis_index("dp")
     far = [1 << b for b in range(2, (shards - 1).bit_length())]
     size, f32 = own * tiles, jnp.float32
@@ -132,44 +148,41 @@
     sub = min(8, rows)
     local = grads.reshape(rows // sub, sub, tiles, LANES).transpose(0, 2, 1, 3).reshape(rows * tiles, LANES)
 
-    dims = (pairs, shards, own, tiles)
-    theirs = swap(local, 1)
-    half = shaped((pairs * (shards // 4) * size, LANES), f32)
+    dims = (shards, own, tiles)
+    theirs = send(local, 1)
+    half = shaped((shards // 2 * size, LANES), f32)
     keep, give, state = call(
         functools.partial(front_kernel, dims), (half, half, shaped((3 * size, LANES), f32)),
         *(pltpu.with_memory_space_constraint(a, pltpu.HBM) for a in (local, master, moment, second)), hbm=True,
         scratch=[pltpu.VMEM(local.shape, f32), pltpu.SemaphoreType.DMA((4,))])
-    theirs_state = swap(state, shards)
+    theirs_state = send(state, shards, 2)
     give, keep = call(functools.partial(sum_kernel, dims), (half, half), theirs, keep, give)
 
     for bit in reversed(far):
         low = (shard & bit) == 0
-        held = jnp.stack([keep, give]).reshape(2, pairs, 2, -1, LANES)
+        held = jnp.stack([keep, give]).reshape(2, 2, 2, -1, LANES)
         mine = jnp.where(low, held[:, :, 0], held[:, :, 1])
         other = jnp.where(low, held[:, :, 1], held[:, :, 0])
-        keep, give = (mine + swap(other, bit)).reshape(2, -1, LANES)
-
-    cross, near, level = swap(give, shards | 2), swap(give, 2), swap(keep, shards)
+        keep, give = (mine + send(other, bit)).reshape(2, -1, LANES)
+
+    cross, near, level = send(give, shards | 2), send(give, 2, shards), send(keep, shards, 2)
     sums = (cross, near, level, keep)
 
     params = call(
-        functools.partial(params_kernel, size), shaped((pairs * size, LANES), jnp.bfloat16),
+        functools.partial(params_kernel, size), shaped((2 * size, LANES), jnp.bfloat16),
         step, *sums, state, theirs_state)
     row = shaped((size, LANES), f32)
     news = call(
         functools.partial(own_kernel, size), (row, row, row), step, *sums, state)
 
-    pieces = [swap(params, bit) for bit in (3, 2, 1)] + [params]
-    block = pairs * 4 * size
+    pieces = [send(params, 3, shards | 1), send(params, 2, shards), send(params, 1), params]
+    block, sub = 8 * own, min(8, 8 * own)
     params = call(
-        functools.partial(order_kernel, pairs, shards, own, tiles), shaped((block, LANES), jnp.bfloat16),
-        *pieces, scratch=[pltpu.VMEM((block, LANES), f32)])
-    near_rows = pairs * 4 * own
-    sub = min(8, near_rows)
-    params = params.reshape(near_rows // sub, tiles, sub, LANES).transpose(0, 2, 1, 3)
-    params = params.reshape(pairs, 4 * own, width)
+        functools.partial(order_kernel, own, tiles), shaped((block * tiles, LANES), jnp.bfloat16),
+        *pieces, scratch=[pltpu.VMEM((block * tiles, LANES), f32)])
+    params = params.reshape(block // sub, tiles, sub, LANES).transpose(0, 2, 1, 3).reshape(2, 4 * own, width)
     for bit in far:
-        low, got = (shard & bit) == 0, swap(params, bit)
+        low, got = (shard & bit) == 0, send(params, bit)
         params = jnp.concatenate([jnp.where(low, params, got), jnp.where(low, got, params)], axis=1)
     return tuple(n.reshape(own, width) for n in news) + (params.reshape(rows, width),)
 

time: 17.2 us -> 17 us (0.988)
  transfers between devices with their start and end apart: 8 -> 8, of which waited for: 5 -> 4; matrix products, arithmetic and copies ran while one was open for 0% -> 0% of each run, Pallas kernels for 10% -> 10%
where the time goes in v2:
time: 17 us; the launch traced here: 16.9 us
  starting transfers between devices  8.58 us (50%)
  waiting for transfers between devices  4.44 us (26%)
  Pallas kernels  2.52 us (15%)
  between operations  1.32 us (8%)
    ppermute x8, starting transfers between devices, send(): lax.ppermute(array, GROUP, [(i, i ^ flip[i & 1]) for i in range(size)])  8.58 us
    ppermute x8, waiting for transfers between devices, send(): lax.ppermute(array, GROUP, [(i, i ^ flip[i & 1]) for i in range(size)])  4.44 us
    pallas_call x5, Pallas kernels, call(): pl.pallas_call(body, out_shape=outs, in_specs=specs, out_specs=jax.tree.m...  2.52 us
  transfers between devices with their start and end apart: 8, of which 4 were waited for; matrix products, arithmetic and copies ran while one was open for 0% of the time, Pallas kernels for 10%

profile of v2, /device:TPU:0, one launch (start us, length us, event | category | flops | bytes accessed | tf_op | source)
XLA Modules:
  0.0 16.9 jit_solution(15131504383182244218)
XLA Ops:
  0.6 0.5 %collective-permute-start = (f32[448,128]{1,0:T(8,128)}, f32[448,128]{1,0:T(8,128)S(1)}, u32[]{:S(2)}, u32[]{:S(2)}) collective-permute-start(f32[448,128]{1,0:T(8,128)} %bitcast.16), channel_id=1, source_target_pairs={{0,1},{1,0},{2,3},{3,2},{16,17},{17,16},{18,19},{19,18},{4,5},{5,4... | collective-permute-start | bytes 688136 | tf_op jit(solution)/shard_map/ppermute | solution.py:18
  1.1 1.0 %shard_map.84 = (f32[112,128]{1,0:T(8,128)S(1)}, f32[112,128]{1,0:T(8,128)S(1)}, f32[168,128]{1,0:T(8,128)S(1)}) custom-call(f32[448,128]{1,0:T(8,128)} %bitcast.17, f32[56,128]{1,0:T(8,128)} %bitcast.19, f32[56,128]{1,0:T(8,128)} %bitcast.20, f32[56,128]{1,0:T(8,128)} %bitcast.21), custom_call_target="tpu_custom_call" | custom-call | tf_op jit(solution)/shard_map/pallas_call | solution.py:128
  2.2 2.6 %collective-permute-start.4 = (f32[168,128]{1,0:T(8,128)S(1)}, f32[168,128]{1,0:T(8,128)S(1)}, u32[]{:S(2)}, u32[]{:S(2)}) collective-permute-start(f32[168,128]{1,0:T(8,128)S(1)} %get-tuple-element.16.state), channel_id=1, source_target_pairs={{0,16},{1,3},{2,18},{3,1},{16,0},{17,19},{18,2},{19,17},{4,20},{5,... | collective-permute-start | bytes 258056 | tf_op jit(solution)/shard_map/ppermute | solution.py:18
  4.8 0.0 collective-permute-done.theirs
  4.8 0.7 %collective-permute-start.3 = (f32[112,128]{1,0:T(8,128)S(1)}, f32[112,128]{1,0:T(8,128)S(1)}, u32[]{:S(2)}, u32[]{:S(2)}) collective-permute-start(f32[112,128]{1,0:T(8,128)S(1)} %get-tuple-element.15.keep), channel_id=1, source_target_pairs={{0,16},{1,3},{2,18},{3,1},{16,0},{17,19},{18,2},{19,17},{4,20},{5,... | collective-permute-start | bytes 172040 | tf_op jit(solution)/shard_map/ppermute | solution.py:18
  5.5 2.4 %collective-permute-start.1 = (f32[112,128]{1,0:T(8,128)S(1)}, f32[112,128]{1,0:T(8,128)S(1)}, u32[]{:S(2)}, u32[]{:S(2)}) collective-permute-start(f32[112,128]{1,0:T(8,128)S(1)} %get-tuple-element.14), channel_id=1, source_target_pairs={{0,18},{1,19},{2,16},{3,17},{16,2},{17,3},{18,0},{19,1},{4,22},{5,... | collective-permute-start | bytes 172040 | tf_op jit(solution)/shard_map/ppermute | solution.py:18
  7.8 0.5 %collective-permute-start.2 = (f32[112,128]{1,0:T(8,128)S(1)}, f32[112,128]{1,0:T(8,128)S(1)}, u32[]{:S(2)}, u32[]{:S(2)}) collective-permute-start(f32[112,128]{1,0:T(8,128)S(1)} %get-tuple-element.14), channel_id=1, source_target_pairs={{0,2},{1,17},{2,0},{3,19},{16,18},{17,1},{18,16},{19,3},{4,6},{5,2... | collective-permute-start | bytes 172040 | tf_op jit(solution)/shard_map/ppermute | solution.py:18
  9.0 0.0 collective-permute-done.4.theirs_state
  9.0 0.0 collective-permute-done.3.level
  9.1 1.5 %collective-permute-done.1.cross = f32[112,128]{1,0:T(8,128)S(1)} collective-permute-done((f32[112,128]{1,0:T(8,128)S(1)}, f32[112,128]{1,0:T(8,128)S(1)}, u32[]{:S(2)}, u32[]{:S(2)}) %collective-permute-start.1) | collective-permute-done | bytes 57376 | tf_op jit(solution)/shard_map/ppermute | solution.py:18
  10.6 1.4 %collective-permute-done.2.near = f32[112,128]{1,0:T(8,128)S(1)} collective-permute-done((f32[112,128]{1,0:T(8,128)S(1)}, f32[112,128]{1,0:T(8,128)S(1)}, u32[]{:S(2)}, u32[]{:S(2)}) %collective-permute-start.2) | collective-permute-done | bytes 57376 | tf_op jit(solution)/shard_map/ppermute | solution.py:18
  12.0 0.1 shard_map.87.refs_3_
  12.1 0.2 collective-permute-start.5
  12.2 0.6 %collective-permute-start.6 = (bf16[112,128]{1,0:T(8,128)(2,1)S(1)}, bf16[112,128]{1,0:T(8,128)(2,1)S(1)}, u32[]{:S(2)}, u32[]{:S(2)}) collective-permute-start(bf16[112,128]{1,0:T(8,128)(2,1)S(1)} %shard_map.87.refs_3_), channel_id=1, source_target_pairs={{0,2},{1,17},{2,0},{3,19},{16,18},{17,1},{18,16},{19,3},{4,6},{5,2... | collective-permute-start | bytes 86024 | tf_op jit(solution)/shard_map/ppermute | solution.py:18
  12.8 1.2 %collective-permute-start.7 = (bf16[112,128]{1,0:T(8,128)(2,1)S(1)}, bf16[112,128]{1,0:T(8,128)(2,1)S(1)}, u32[]{:S(2)}, u32[]{:S(2)}) collective-permute-start(bf16[112,128]{1,0:T(8,128)(2,1)S(1)} %shard_map.87.refs_3_), channel_id=1, source_target_pairs={{0,1},{1,0},{2,3},{3,2},{16,17},{17,16},{18,19},{19,18},{4,5},{5,4... | collective-permute-start | bytes 86024 | tf_op jit(solution)/shard_map/ppermute | solution.py:18
  14.0 0.7 %shard_map.86 = (f32[56,128]{1,0:T(8,128)}, f32[56,128]{1,0:T(8,128)}, f32[56,128]{1,0:T(8,128)}) custom-call(s32[1]{0:T(128)S(6)} %copy.9.step_ref, f32[112,128]{1,0:T(8,128)S(1)} %collective-permute-done.1.cross, f32[112,128]{1,0:T(8,128)S(1)} %collective-permute-done.2.near, f32[112,128]{1,0:T(8,128)S(1)} %collective-permute-done.3.level, ...), custom_call_target="tpu_custom_call" | custom-call | tf_op jit(solution)/shard_map/pallas_call | solution.py:128
  14.7 0.8 %collective-permute-done.5.refs_0_ = bf16[112,128]{1,0:T(8,128)(2,1)S(1)} collective-permute-done((bf16[112,128]{1,0:T(8,128)(2,1)S(1)}, bf16[112,128]{1,0:T(8,128)(2,1)S(1)}, u32[]{:S(2)}, u32[]{:S(2)}) %collective-permute-start.5) | collective-permute-done | bytes 28704 | tf_op jit(solution)/shard_map/ppermute | solution.py:18
  15.4 0.7 %collective-permute-done.6.refs_1_ = bf16[112,128]{1,0:T(8,128)(2,1)S(1)} collective-permute-done((bf16[112,128]{1,0:T(8,128)(2,1)S(1)}, bf16[112,128]{1,0:T(8,128)(2,1)S(1)}, u32[]{:S(2)}, u32[]{:S(2)}) %collective-permute-start.6) | collective-permute-done | bytes 28704 | tf_op jit(solution)/shard_map/ppermute | solution.py:18
  16.1 0.0 collective-permute-done.7.refs_2_
  16.1 0.7 %shard_map.88 = bf16[448,128]{1,0:T(8,128)(2,1)} custom-call(bf16[112,128]{1,0:T(8,128)(2,1)S(1)} %collective-permute-done.5.refs_0_, bf16[112,128]{1,0:T(8,128)(2,1)S(1)} %collective-permute-done.6.refs_1_, bf16[112,128]{1,0:T(8,128)(2,1)S(1)} %collective-permute-done.7.refs_2_, bf16[112,128]{1,0:T(8,128)(2,1)S(1)} %shard_map.87.refs_3_), custom_call_target="tpu_custom_call" | custom-call | tf_op jit(solution)/shard_map/pallas_call | solution.py:128
  (1 shorter events, 0.0 us)
Async XLA Ops:
  0.6 4.1 %collective-permute-start = (f32[448,128]{1,0:T(8,128)}, f32[448,128]{1,0:T(8,128)S(1)}, u32[]{:S(2)}, u32[]{:S(2)}) collective-permute-start(f32[448,128]{1,0:T(8,128)} %bitcast.16), channel_id=1, source_target_pairs={{0,1},{1,0},{2,3},{3,2},{16,17},{17,16},{18,19},{19,18},{4,5},{5,4... | collective-permute-start | bytes 688136 | tf_op jit(solution)/shard_map/ppermute | solution.py:18
  2.2 6.9 %collective-permute-start.4 = (f32[168,128]{1,0:T(8,128)S(1)}, f32[168,128]{1,0:T(8,128)S(1)}, u32[]{:S(2)}, u32[]{:S(2)}) collective-permute-start(f32[168,128]{1,0:T(8,128)S(1)} %get-tuple-element.16.state), channel_id=1, source_target_pairs={{0,16},{1,3},{2,18},{3,1},{16,0},{17,19},{18,2},{19,17},{4,20},{5,... | collective-permute-start | bytes 258056 | tf_op jit(solution)/shard_map/ppermute | solution.py:18
  4.8 4.2 %collective-permute-start.3 = (f32[112,128]{1,0:T(8,128)S(1)}, f32[112,128]{1,0:T(8,128)S(1)}, u32[]{:S(2)}, u32[]{:S(2)}) collective-permute-start(f32[112,128]{1,0:T(8,128)S(1)} %get-tuple-element.15.keep), channel_id=1, source_target_pairs={{0,16},{1,3},{2,18},{3,1},{16,0},{17,19},{18,2},{19,17},{4,20},{5,... | collective-permute-start | bytes 172040 | tf_op jit(solution)/shard_map/ppermute | solution.py:18
  5.5 5.1 %collective-permute-start.1 = (f32[112,128]{1,0:T(8,128)S(1)}, f32[112,128]{1,0:T(8,128)S(1)}, u32[]{:S(2)}, u32[]{:S(2)}) collective-permute-start(f32[112,128]{1,0:T(8,128)S(1)} %get-tuple-element.14), channel_id=1, source_target_pairs={{0,18},{1,19},{2,16},{3,17},{16,2},{17,3},{18,0},{19,1},{4,22},{5,... | collective-permute-start | bytes 172040 | tf_op jit(solution)/shard_map/ppermute | solution.py:18
  7.8 4.2 %collective-permute-start.2 = (f32[112,128]{1,0:T(8,128)S(1)}, f32[112,128]{1,0:T(8,128)S(1)}, u32[]{:S(2)}, u32[]{:S(2)}) collective-permute-start(f32[112,128]{1,0:T(8,128)S(1)} %get-tuple-element.14), channel_id=1, source_target_pairs={{0,2},{1,17},{2,0},{3,19},{16,18},{17,1},{18,16},{19,3},{4,6},{5,2... | collective-permute-start | bytes 172040 | tf_op jit(solution)/shard_map/ppermute | solution.py:18
  12.1 3.3 %collective-permute-start.5 = (bf16[112,128]{1,0:T(8,128)(2,1)S(1)}, bf16[112,128]{1,0:T(8,128)(2,1)S(1)}, u32[]{:S(2)}, u32[]{:S(2)}) collective-permute-start(bf16[112,128]{1,0:T(8,128)(2,1)S(1)} %shard_map.87.refs_3_), channel_id=1, source_target_pairs={{0,3},{1,16},{2,1},{3,18},{16,19},{17,0},{18,17},{19,2},{4,7},{5,2... | collective-permute-start | bytes 86024 | tf_op jit(solution)/shard_map/ppermute | solution.py:18
  12.2 3.9 %collective-permute-start.6 = (bf16[112,128]{1,0:T(8,128)(2,1)S(1)}, bf16[112,128]{1,0:T(8,128)(2,1)S(1)}, u32[]{:S(2)}, u32[]{:S(2)}) collective-permute-start(bf16[112,128]{1,0:T(8,128)(2,1)S(1)} %shard_map.87.refs_3_), channel_id=1, source_target_pairs={{0,2},{1,17},{2,0},{3,19},{16,18},{17,1},{18,16},{19,3},{4,6},{5,2... | collective-permute-start | bytes 86024 | tf_op jit(solution)/shard_map/ppermute | solution.py:18
  12.8 3.3 %collective-permute-start.7 = (bf16[112,128]{1,0:T(8,128)(2,1)S(1)}, bf16[112,128]{1,0:T(8,128)(2,1)S(1)}, u32[]{:S(2)}, u32[]{:S(2)}) collective-permute-start(bf16[112,128]{1,0:T(8,128)(2,1)S(1)} %shard_map.87.refs_3_), channel_id=1, source_target_pairs={{0,1},{1,0},{2,3},{3,2},{16,17},{17,16},{18,19},{19,18},{4,5},{5,4... | collective-permute-start | bytes 86024 | tf_op jit(solution)/shard_map/ppermute | solution.py:18

commit v3 on v2

--- a/solution.py
+++ b/solution.py
@@ -30,39 +30,42 @@
 
 
 def my_rows(shards, own, tiles):
-    core = lax.axis_index("dp") & 1
-    rows, i = 2 * shards * own, 0
+    core, i = lax.axis_index("dp") & 1, 0
     for slot in range(2):
         kept, given = place(slot, 0), place(slot, 1)
         for far in range(shards // 4):
             for o in range(own):
-                at = [
-                    row_at((pair * shards + far * 4 + near * 2 + core) * own + o, tiles, rows)
-                    for pair, near in (kept, given)
+                yield pl.ds(i * tiles, tiles), [
+                    (pair * shards + far * 4 + near * 2 + core) * own + o for pair, near in (kept, given)
                 ]
-                yield slice(i * tiles, (i + 1) * tiles), at
                 i += 1
 
 
-def front_kernel(dims, local, master, moment, second, keep_ref, give_ref, state_ref, held, sems):
-    size = master.shape[0]
-    copies = [pltpu.make_async_copy(local, held, sems.at[3])]
+def front_kernel(dims, local, master, moment, second, keep_ref, give_ref, state_ref, sems):
+    size, tiles, sub = master.shape[0], dims[2], local.shape[1]
+    copies = []
     for i, source in enumerate((master, moment, second)):
-        to = state_ref.at[pl.ds(i * size, size), :]
-        copies.append(pltpu.make_async_copy(source, to, sems.at[i]))
+        copies.append((source, state_ref.at[pl.ds(i * size, size)]))
+    for to, rows in my_rows(*dims):
+        for row, out_ref in zip(rows, (keep_ref, give_ref)):
+            block = pl.ds((row // sub) * tiles, tiles)
+            copies.append((local.at[block, row % sub], out_ref.at[to]))
+    copies = [pltpu.make_async_copy(*c, sems.at[i]) for i, c in enumerate(copies)]
     for copy in copies:
         copy.start()
     for copy in copies:
         copy.wait()
-    for to, (mine, other) in my_rows(*dims):
-        keep_ref[to, :] = held[mine, :]
-        give_ref[to, :] = held[other, :]
-
-
-def sum_kernel(dims, theirs, own_keep, own_give, give_ref, keep_ref):
-    for to, (mine, other) in my_rows(*dims):
-        keep_ref[to, :] = own_keep[to, :] + theirs[mine, :]
-        give_ref[to, :] = own_give[to, :] + theirs[other, :]
+
+
+def sum_kernel(dims, theirs, own_keep, own_give, cross_ref, near_ref, level_ref, keep_ref):
+    tiles, rows = dims[2], 2 * dims[0] * dims[1]
+    for to, (kept, given) in my_rows(*dims):
+        keep = own_keep[to, :] + theirs[row_at(kept, tiles, rows), :]
+        keep_ref[to, :] = keep
+        level_ref[to, :] = keep
+        give = own_give[to, :] + theirs[row_at(given, tiles, rows), :]
+        cross_ref[to, :] = give
+        near_ref[to, :] = give
 
 
 def adam(total, master, moment, second, count):
@@ -151,21 +154,25 @@
     dims = (shards, own, tiles)
     theirs = send(local, 1)
     half = shaped((shards // 2 * size, LANES), f32)
-    keep, give, state = call(
-        functools.partial(front_kernel, dims), (half, half, shaped((3 * size, LANES), f32)),
-        *(pltpu.with_memory_space_constraint(a, pltpu.HBM) for a in (local, master, moment, second)), hbm=True,
-        scratch=[pltpu.VMEM(local.shape, f32), pltpu.SemaphoreType.DMA((4,))])
+    blocks = local.reshape(rows // sub * tiles, sub, 1, LANES)
+    flat = [a.reshape(size, 1, LANES) for a in (master, moment, second)]
+    picked = shaped((half.shape[0], 1, LANES), f32)
+    keep, give, state = (a.reshape(-1, LANES) for a in call(
+        functools.partial(front_kernel, dims), (picked, picked, shaped((3 * size, 1, LANES), f32)),
+        *(pltpu.with_memory_space_constraint(a, pltpu.HBM) for a in (blocks, *flat)), hbm=True,
+        scratch=[pltpu.SemaphoreType.DMA((3 + 2 * (half.shape[0] // tiles),))]))
     theirs_state = send(state, shards, 2)
-    give, keep = call(functools.partial(sum_kernel, dims), (half, half), theirs, keep, give)
+    to_cross, to_near, to_level, keep = call(functools.partial(sum_kernel, dims), (half, half, half, half), theirs, keep, give)
 
     for bit in reversed(far):
         low = (shard & bit) == 0
-        held = jnp.stack([keep, give]).reshape(2, 2, 2, -1, LANES)
+        held = jnp.stack([keep, to_near]).reshape(2, 2, 2, -1, LANES)
         mine = jnp.where(low, held[:, :, 0], held[:, :, 1])
         other = jnp.where(low, held[:, :, 1], held[:, :, 0])
-        keep, give = (mine + send(other, bit)).reshape(2, -1, LANES)
-
-    cross, near, level = send(give, shards | 2), send(give, 2, shards), send(keep, shards, 2)
+        keep, to_near = (mine + send(other, bit)).reshape(2, -1, LANES)
+        to_cross, to_level = to_near, keep
+
+    cross, near, level = send(to_cross, shards | 2), send(to_near, 2, shards), send(to_level, shards, 2)
     sums = (cross, near, level, keep)
 
     params = call(

time: 17 us -> 16.3 us (0.959)
  waiting for transfers between devices: 4.44 us -> 3.78 us
    ppermute x8, waiting for transfers between devices: 4.44 us -> 3.78 us  [send(): lax.ppermute(array, GROUP, [(i, i ^ flip[i & 1]) for i in range(size)])]
  transfers between devices with their start and end apart: 8 -> 8, of which waited for: 4 -> 5; matrix products, arithmetic and copies ran while one was open for 0% -> 0% of each run, Pallas kernels for 10% -> 10%
where the time goes in v3:
time: 16.3 us; the launch traced here: 16.1 us
  starting transfers between devices  8.59 us (53%)
  waiting for transfers between devices  3.78 us (23%)
  Pallas kernels  2.42 us (15%)
  between operations  1.31 us (8%)
    ppermute x8, starting transfers between devices, send(): lax.ppermute(array, GROUP, [(i, i ^ flip[i & 1]) for i in range(size)])  8.59 us
    ppermute x8, waiting for transfers between devices, send(): lax.ppermute(array, GROUP, [(i, i ^ flip[i & 1]) for i in range(size)])  3.78 us
    pallas_call x5, Pallas kernels, call(): pl.pallas_call(body, out_shape=outs, in_specs=specs, out_specs=jax.tree.m...  2.42 us
  transfers between devices with their start and end apart: 8, of which 5 were waited for; matrix products, arithmetic and copies ran while one was open for 0% of the time, Pallas kernels for 10%

profile of v3, /device:TPU:0, one launch (start us, length us, event | category | flops | bytes accessed | tf_op | source)
XLA Modules:
  0.0 16.1 jit_solution(9641856804055467861)
XLA Ops:
  0.6 0.5 %collective-permute-start = (f32[448,128]{1,0:T(8,128)}, f32[448,128]{1,0:T(8,128)S(1)}, u32[]{:S(2)}, u32[]{:S(2)}) collective-permute-start(f32[448,128]{1,0:T(8,128)} %bitcast.26), channel_id=1, source_target_pairs={{0,1},{1,0},{2,3},{3,2},{16,17},{17,16},{18,19},{19,18},{4,5},{5,4... | collective-permute-start | bytes 688136 | tf_op jit(solution)/shard_map/ppermute | solution.py:18
  1.1 0.9 %shard_map.84 = (f32[112,1,128]{2,1,0:T(1,128)S(1)}, f32[112,1,128]{2,1,0:T(1,128)S(1)}, f32[168,1,128]{2,1,0:T(1,128)S(1)}) custom-call(f32[56,8,1,128]{3,2,1,0:T(1,128)} %bitcast.27, f32[56,1,128]{2,1,0:T(1,128)} %bitcast.29, f32[56,1,128]{2,1,0:T(1,128)} %bitcast.30, f32[56,1,128]{2,1,0:T(1,128)} %bitcast.31), custom_call_target="tpu_custom_call" | custom-call | tf_op jit(solution)/shard_map/pallas_call | solution.py:131
  2.1 2.6 %collective-permute-start.4 = (f32[168,128]{1,0:T(8,128)S(1)}, f32[168,128]{1,0:T(8,128)S(1)}, u32[]{:S(2)}, u32[]{:S(2)}) collective-permute-start(f32[168,128]{1,0:T(8,128)S(1)} %bitcast.21), channel_id=1, source_target_pairs={{0,16},{1,3},{2,18},{3,1},{16,0},{17,19},{18,2},{19,17},{4,20},{5,... | collective-permute-start | bytes 258056 | tf_op jit(solution)/shard_map/ppermute | solution.py:18
  4.7 0.0 collective-permute-done.theirs
  4.7 1.7 %collective-permute-start.1 = (f32[112,128]{1,0:T(8,128)S(1)}, f32[112,128]{1,0:T(8,128)S(1)}, u32[]{:S(2)}, u32[]{:S(2)}) collective-permute-start(f32[112,128]{1,0:T(8,128)S(1)} %get-tuple-element.16), channel_id=1, source_target_pairs={{0,18},{1,19},{2,16},{3,17},{16,2},{17,3},{18,0},{19,1},{4,22},{5,... | collective-permute-start | bytes 172040 | tf_op jit(solution)/shard_map/ppermute | solution.py:18
  6.4 0.5 %collective-permute-start.2 = (f32[112,128]{1,0:T(8,128)S(1)}, f32[112,128]{1,0:T(8,128)S(1)}, u32[]{:S(2)}, u32[]{:S(2)}) collective-permute-start(f32[112,128]{1,0:T(8,128)S(1)} %get-tuple-element.17), channel_id=1, source_target_pairs={{0,2},{1,17},{2,0},{3,19},{16,18},{17,1},{18,16},{19,3},{4,6},{5,2... | collective-permute-start | bytes 172040 | tf_op jit(solution)/shard_map/ppermute | solution.py:18
  6.9 1.3 %collective-permute-start.3 = (f32[112,128]{1,0:T(8,128)S(1)}, f32[112,128]{1,0:T(8,128)S(1)}, u32[]{:S(2)}, u32[]{:S(2)}) collective-permute-start(f32[112,128]{1,0:T(8,128)S(1)} %get-tuple-element.18), channel_id=1, source_target_pairs={{0,16},{1,3},{2,18},{3,1},{16,0},{17,19},{18,2},{19,17},{4,20},{5,... | collective-permute-start | bytes 172040 | tf_op jit(solution)/shard_map/ppermute | solution.py:18
  8.9 0.0 collective-permute-done.4.theirs_state
  8.9 1.0 %collective-permute-done.1.cross = f32[112,128]{1,0:T(8,128)S(1)} collective-permute-done((f32[112,128]{1,0:T(8,128)S(1)}, f32[112,128]{1,0:T(8,128)S(1)}, u32[]{:S(2)}, u32[]{:S(2)}) %collective-permute-start.1) | collective-permute-done | bytes 57376 | tf_op jit(solution)/shard_map/ppermute | solution.py:18
  9.9 1.0 %collective-permute-done.2.near = f32[112,128]{1,0:T(8,128)S(1)} collective-permute-done((f32[112,128]{1,0:T(8,128)S(1)}, f32[112,128]{1,0:T(8,128)S(1)}, u32[]{:S(2)}, u32[]{:S(2)}) %collective-permute-start.2) | collective-permute-done | bytes 57376 | tf_op jit(solution)/shard_map/ppermute | solution.py:18
  10.9 0.2 %collective-permute-done.3.level = f32[112,128]{1,0:T(8,128)S(1)} collective-permute-done((f32[112,128]{1,0:T(8,128)S(1)}, f32[112,128]{1,0:T(8,128)S(1)}, u32[]{:S(2)}, u32[]{:S(2)}) %collective-permute-start.3) | collective-permute-done | bytes 57376 | tf_op jit(solution)/shard_map/ppermute | solution.py:18
  11.1 0.1 shard_map.87.refs_3_
  11.2 0.3 %collective-permute-start.5 = (bf16[112,128]{1,0:T(8,128)(2,1)S(1)}, bf16[112,128]{1,0:T(8,128)(2,1)S(1)}, u32[]{:S(2)}, u32[]{:S(2)}) collective-permute-start(bf16[112,128]{1,0:T(8,128)(2,1)S(1)} %shard_map.87.refs_3_), channel_id=1, source_target_pairs={{0,3},{1,16},{2,1},{3,18},{16,19},{17,0},{18,17},{19,2},{4,7},{5,2... | collective-permute-start | bytes 86024 | tf_op jit(solution)/shard_map/ppermute | solution.py:18
  11.5 1.3 %collective-permute-start.6 = (bf16[112,128]{1,0:T(8,128)(2,1)S(1)}, bf16[112,128]{1,0:T(8,128)(2,1)S(1)}, u32[]{:S(2)}, u32[]{:S(2)}) collective-permute-start(bf16[112,128]{1,0:T(8,128)(2,1)S(1)} %shard_map.87.refs_3_), channel_id=1, source_target_pairs={{0,2},{1,17},{2,0},{3,19},{16,18},{17,1},{18,16},{19,3},{4,6},{5,2... | collective-permute-start | bytes 86024 | tf_op jit(solution)/shard_map/ppermute | solution.py:18
  12.8 0.3 %collective-permute-start.7 = (bf16[112,128]{1,0:T(8,128)(2,1)S(1)}, bf16[112,128]{1,0:T(8,128)(2,1)S(1)}, u32[]{:S(2)}, u32[]{:S(2)}) collective-permute-start(bf16[112,128]{1,0:T(8,128)(2,1)S(1)} %shard_map.87.refs_3_), channel_id=1, source_target_pairs={{0,1},{1,0},{2,3},{3,2},{16,17},{17,16},{18,19},{19,18},{4,5},{5,4... | collective-permute-start | bytes 86024 | tf_op jit(solution)/shard_map/ppermute | solution.py:18
  13.1 0.7 %shard_map.86 = (f32[56,128]{1,0:T(8,128)}, f32[56,128]{1,0:T(8,128)}, f32[56,128]{1,0:T(8,128)}) custom-call(s32[1]{0:T(128)S(6)} %copy.9.step_ref, f32[112,128]{1,0:T(8,128)S(1)} %collective-permute-done.1.cross, f32[112,128]{1,0:T(8,128)S(1)} %collective-permute-done.2.near, f32[112,128]{1,0:T(8,128)S(1)} %collective-permute-done.3.level, ...), custom_call_target="tpu_custom_call" | custom-call | tf_op jit(solution)/shard_map/pallas_call | solution.py:131
  13.8 0.8 %collective-permute-done.5.refs_0_ = bf16[112,128]{1,0:T(8,128)(2,1)S(1)} collective-permute-done((bf16[112,128]{1,0:T(8,128)(2,1)S(1)}, bf16[112,128]{1,0:T(8,128)(2,1)S(1)}, u32[]{:S(2)}, u32[]{:S(2)}) %collective-permute-start.5) | collective-permute-done | bytes 28704 | tf_op jit(solution)/shard_map/ppermute | solution.py:18
  14.5 0.8 %collective-permute-done.6.refs_1_ = bf16[112,128]{1,0:T(8,128)(2,1)S(1)} collective-permute-done((bf16[112,128]{1,0:T(8,128)(2,1)S(1)}, bf16[112,128]{1,0:T(8,128)(2,1)S(1)}, u32[]{:S(2)}, u32[]{:S(2)}) %collective-permute-start.6) | collective-permute-done | bytes 28704 | tf_op jit(solution)/shard_map/ppermute | solution.py:18
  15.3 0.0 collective-permute-done.7.refs_2_
  15.4 0.7 %shard_map.88 = bf16[448,128]{1,0:T(8,128)(2,1)} custom-call(bf16[112,128]{1,0:T(8,128)(2,1)S(1)} %collective-permute-done.5.refs_0_, bf16[112,128]{1,0:T(8,128)(2,1)S(1)} %collective-permute-done.6.refs_1_, bf16[112,128]{1,0:T(8,128)(2,1)S(1)} %collective-permute-done.7.refs_2_, bf16[112,128]{1,0:T(8,128)(2,1)S(1)} %shard_map.87.refs_3_), custom_call_target="tpu_custom_call" | custom-call | tf_op jit(solution)/shard_map/pallas_call | solution.py:131
  (1 shorter events, 0.0 us)
Async XLA Ops:
  0.6 4.0 %collective-permute-start = (f32[448,128]{1,0:T(8,128)}, f32[448,128]{1,0:T(8,128)S(1)}, u32[]{:S(2)}, u32[]{:S(2)}) collective-permute-start(f32[448,128]{1,0:T(8,128)} %bitcast.26), channel_id=1, source_target_pairs={{0,1},{1,0},{2,3},{3,2},{16,17},{17,16},{18,19},{19,18},{4,5},{5,4... | collective-permute-start | bytes 688136 | tf_op jit(solution)/shard_map/ppermute | solution.py:18
  2.1 6.9 %collective-permute-start.4 = (f32[168,128]{1,0:T(8,128)S(1)}, f32[168,128]{1,0:T(8,128)S(1)}, u32[]{:S(2)}, u32[]{:S(2)}) collective-permute-start(f32[168,128]{1,0:T(8,128)S(1)} %bitcast.21), channel_id=1, source_target_pairs={{0,16},{1,3},{2,18},{3,1},{16,0},{17,19},{18,2},{19,17},{4,20},{5,... | collective-permute-start | bytes 258056 | tf_op jit(solution)/shard_map/ppermute | solution.py:18
  4.7 5.2 %collective-permute-start.1 = (f32[112,128]{1,0:T(8,128)S(1)}, f32[112,128]{1,0:T(8,128)S(1)}, u32[]{:S(2)}, u32[]{:S(2)}) collective-permute-start(f32[112,128]{1,0:T(8,128)S(1)} %get-tuple-element.16), channel_id=1, source_target_pairs={{0,18},{1,19},{2,16},{3,17},{16,2},{17,3},{18,0},{19,1},{4,22},{5,... | collective-permute-start | bytes 172040 | tf_op jit(solution)/shard_map/ppermute | solution.py:18
  6.4 4.5 %collective-permute-start.2 = (f32[112,128]{1,0:T(8,128)S(1)}, f32[112,128]{1,0:T(8,128)S(1)}, u32[]{:S(2)}, u32[]{:S(2)}) collective-permute-start(f32[112,128]{1,0:T(8,128)S(1)} %get-tuple-element.17), channel_id=1, source_target_pairs={{0,2},{1,17},{2,0},{3,19},{16,18},{17,1},{18,16},{19,3},{4,6},{5,2... | collective-permute-start | bytes 172040 | tf_op jit(solution)/shard_map/ppermute | solution.py:18
  6.9 4.2 %collective-permute-start.3 = (f32[112,128]{1,0:T(8,128)S(1)}, f32[112,128]{1,0:T(8,128)S(1)}, u32[]{:S(2)}, u32[]{:S(2)}) collective-permute-start(f32[112,128]{1,0:T(8,128)S(1)} %get-tuple-element.18), channel_id=1, source_target_pairs={{0,16},{1,3},{2,18},{3,1},{16,0},{17,19},{18,2},{19,17},{4,20},{5,... | collective-permute-start | bytes 172040 | tf_op jit(solution)/shard_map/ppermute | solution.py:18
  11.2 3.3 %collective-permute-start.5 = (bf16[112,128]{1,0:T(8,128)(2,1)S(1)}, bf16[112,128]{1,0:T(8,128)(2,1)S(1)}, u32[]{:S(2)}, u32[]{:S(2)}) collective-permute-start(bf16[112,128]{1,0:T(8,128)(2,1)S(1)} %shard_map.87.refs_3_), channel_id=1, source_target_pairs={{0,3},{1,16},{2,1},{3,18},{16,19},{17,0},{18,17},{19,2},{4,7},{5,2... | collective-permute-start | bytes 86024 | tf_op jit(solution)/shard_map/ppermute | solution.py:18
  11.5 3.9 %collective-permute-start.6 = (bf16[112,128]{1,0:T(8,128)(2,1)S(1)}, bf16[112,128]{1,0:T(8,128)(2,1)S(1)}, u32[]{:S(2)}, u32[]{:S(2)}) collective-permute-start(bf16[112,128]{1,0:T(8,128)(2,1)S(1)} %shard_map.87.refs_3_), channel_id=1, source_target_pairs={{0,2},{1,17},{2,0},{3,19},{16,18},{17,1},{18,16},{19,3},{4,6},{5,2... | collective-permute-start | bytes 86024 | tf_op jit(solution)/shard_map/ppermute | solution.py:18
  12.8 2.5 %collective-permute-start.7 = (bf16[112,128]{1,0:T(8,128)(2,1)S(1)}, bf16[112,128]{1,0:T(8,128)(2,1)S(1)}, u32[]{:S(2)}, u32[]{:S(2)}) collective-permute-start(bf16[112,128]{1,0:T(8,128)(2,1)S(1)} %shard_map.87.refs_3_), channel_id=1, source_target_pairs={{0,1},{1,0},{2,3},{3,2},{16,17},{17,16},{18,19},{19,18},{4,5},{5,4... | collective-permute-start | bytes 86024 | tf_op jit(solution)/shard_map/ppermute | solution.py:18

commit v4 on v3

--- a/solution.py
+++ b/solution.py
@@ -23,31 +23,30 @@
     return pl.ds((row // sub) * (tiles * sub) + row % sub, tiles, stride=sub)
 
 
-def place(slot, other):
-    pair, shard = lax.axis_index("pair"), lax.axis_index("dp")
-    core, near = shard & 1, (shard >> 1) & 1
+def place(core, slot, other):
+    pair, near = lax.axis_index("pair"), (lax.axis_index("dp") >> 1) & 1
     return pair ^ (slot * (1 - core)) ^ (other * core), near ^ (slot * core) ^ (other * (1 - core))
 
 
 def my_rows(shards, own, tiles):
     core, i = lax.axis_index("dp") & 1, 0
     for slot in range(2):
-        kept, given = place(slot, 0), place(slot, 1)
+        places = [(*place(c, slot, other), c) for c, other in ((core, 0), (1 - core, 0), (1 - core, 1))]
         for far in range(shards // 4):
             for o in range(own):
                 yield pl.ds(i * tiles, tiles), [
-                    (pair * shards + far * 4 + near * 2 + core) * own + o for pair, near in (kept, given)
+                    (pair * shards + far * 4 + near * 2 + c) * own + o for pair, near, c in places
                 ]
                 i += 1
 
 
-def front_kernel(dims, local, master, moment, second, keep_ref, give_ref, state_ref, sems):
+def front_kernel(dims, local, master, moment, second, keep_ref, level_ref, give_ref, state_ref, sems):
     size, tiles, sub = master.shape[0], dims[2], local.shape[1]
     copies = []
     for i, source in enumerate((master, moment, second)):
         copies.append((source, state_ref.at[pl.ds(i * size, size)]))
     for to, rows in my_rows(*dims):
-        for row, out_ref in zip(rows, (keep_ref, give_ref)):
+        for row, out_ref in zip(rows, (keep_ref, level_ref, give_ref)):
             block = pl.ds((row // sub) * tiles, tiles)
             copies.append((local.at[block, row % sub], out_ref.at[to]))
     copies = [pltpu.make_async_copy(*c, sems.at[i]) for i, c in enumerate(copies)]
@@ -57,12 +56,11 @@
         copy.wait()
 
 
-def sum_kernel(dims, theirs, own_keep, own_give, cross_ref, near_ref, level_ref, keep_ref):
+def sum_kernel(dims, theirs, own_keep, own_level, own_give, cross_ref, near_ref, level_ref, keep_ref):
     tiles, rows = dims[2], 2 * dims[0] * dims[1]
-    for to, (kept, given) in my_rows(*dims):
-        keep = own_keep[to, :] + theirs[row_at(kept, tiles, rows), :]
-        keep_ref[to, :] = keep
-        level_ref[to, :] = keep
+    for to, (kept, level, given) in my_rows(*dims):
+        keep_ref[to, :] = own_keep[to, :] + theirs[row_at(kept, tiles, rows), :]
+        level_ref[to, :] = own_level[to, :] + theirs[row_at(level, tiles, rows), :]
         give = own_give[to, :] + theirs[row_at(given, tiles, rows), :]
         cross_ref[to, :] = give
         near_ref[to, :] = give
@@ -109,8 +107,8 @@
     pair, shard = lax.axis_index("pair"), lax.axis_index("dp")
     core, near = shard & 1, (shard >> 1) & 1
     sources = (
+        (pair ^ core, near ^ (1 - core), core),
         (pair ^ (1 - core), near ^ core, core ^ 1),
-        (pair ^ core, near ^ (1 - core), core),
         (pair, near, core ^ 1),
         (pair, near, core),
     )
@@ -157,22 +155,23 @@
     blocks = local.reshape(rows // sub * tiles, sub, 1, LANES)
     flat = [a.reshape(size, 1, LANES) for a in (master, moment, second)]
     picked = shaped((half.shape[0], 1, LANES), f32)
-    keep, give, state = (a.reshape(-1, LANES) for a in call(
-        functools.partial(front_kernel, dims), (picked, picked, shaped((3 * size, 1, LANES), f32)),
+    *picks, state = (a.reshape(-1, LANES) for a in call(
+        functools.partial(front_kernel, dims), (picked, picked, picked, shaped((3 * size, 1, LANES), f32)),
         *(pltpu.with_memory_space_constraint(a, pltpu.HBM) for a in (blocks, *flat)), hbm=True,
-        scratch=[pltpu.SemaphoreType.DMA((3 + 2 * (half.shape[0] // tiles),))]))
+        scratch=[pltpu.SemaphoreType.DMA((3 + 3 * (half.shape[0] // tiles),))]))
     theirs_state = send(state, shards, 2)
-    to_cross, to_near, to_level, keep = call(functools.partial(sum_kernel, dims), (half, half, half, half), theirs, keep, give)
+    to_cross, to_near, to_level, keep = call(functools.partial(sum_kernel, dims), (half,) * 4, theirs, *picks)
 
     for bit in reversed(far):
         low = (shard & bit) == 0
-        held = jnp.stack([keep, to_near]).reshape(2, 2, 2, -1, LANES)
+        held = jnp.stack([keep, to_level, to_near]).reshape(3, 2, 2, -1, LANES)
         mine = jnp.where(low, held[:, :, 0], held[:, :, 1])
         other = jnp.where(low, held[:, :, 1], held[:, :, 0])
-        keep, to_near = (mine + send(other, bit)).reshape(2, -1, LANES)
-        to_cross, to_level = to_near, keep
-
-    cross, near, level = send(to_cross, shards | 2), send(to_near, 2, shards), send(to_level, shards, 2)
+        keep, to_level, to_near = (mine + send(other, bit)).reshape(3, -1, LANES)
+        to_cross = to_near
+
+    cross = send(to_cross, shards | 3)
+    near, level = send(to_near, shards | 1, 3), send(to_level, 3, shards | 1)
     sums = (cross, near, level, keep)
 
     params = call(
@@ -182,7 +181,7 @@
     news = call(
         functools.partial(own_kernel, size), (row, row, row), step, *sums, state)
 
-    pieces = [send(params, 3, shards | 1), send(params, 2, shards), send(params, 1), params]
+    pieces = [send(params, 2, shards), send(params, 3, shards | 1), send(params, 1), params]
     block, sub = 8 * own, min(8, 8 * own)
     params = call(
         functools.partial(order_kernel, own, tiles), shaped((block * tiles, LANES), jnp.bfloat16),

time: 16.3 us -> 16.5 us (1.012)
  waiting for transfers between devices: 3.78 us -> 3.95 us
    ppermute x8, waiting for transfers between devices: 3.78 us -> 3.95 us  [send(): lax.ppermute(array, GROUP, [(i, i ^ flip[i & 1]) for i in range(size)])]
where the time goes in v4:
time: 16.5 us; the launch traced here: 16.3 us
  starting transfers between devices  8.56 us (52%)
  waiting for transfers between devices  3.95 us (24%)
  Pallas kernels  2.49 us (15%)
  between operations  1.32 us (8%)
    ppermute x8, starting transfers between devices, send(): lax.ppermute(array, GROUP, [(i, i ^ flip[i & 1]) for i in range(size)])  8.56 us
    ppermute x8, waiting for transfers between devices, send(): lax.ppermute(array, GROUP, [(i, i ^ flip[i & 1]) for i in range(size)])  3.95 us
    pallas_call x5, Pallas kernels, call(): pl.pallas_call(body, out_shape=outs, in_specs=specs, out_specs=jax.tree.m...  2.49 us
  transfers between devices with their start and end apart: 8, of which 5 were waited for; matrix products, arithmetic and copies ran while one was open for 0% of the time, Pallas kernels for 10%

profile of v4, /device:TPU:0, one launch (start us, length us, event | category | flops | bytes accessed | tf_op | source)
XLA Modules:
  0.0 16.3 jit_solution(723647787542220302)
XLA Ops:
  0.6 0.5 %collective-permute-start = (f32[448,128]{1,0:T(8,128)}, f32[448,128]{1,0:T(8,128)S(1)}, u32[]{:S(2)}, u32[]{:S(2)}) collective-permute-start(f32[448,128]{1,0:T(8,128)} %bitcast.28), channel_id=1, source_target_pairs={{0,1},{1,0},{2,3},{3,2},{16,17},{17,16},{18,19},{19,18},{4,5},{5,4... | collective-permute-start | bytes 688136 | tf_op jit(solution)/shard_map/ppermute | solution.py:18
  1.1 1.0 %shard_map.84 = (f32[112,1,128]{2,1,0:T(1,128)S(1)}, f32[112,1,128]{2,1,0:T(1,128)S(1)}, f32[112,1,128]{2,1,0:T(1,128)S(1)}, f32[168,1,128]{2,1,0:T(1,128)S(1)}) custom-call(f32[56,8,1,128]{3,2,1,0:T(1,128)} %bitcast.29, f32[56,1,128]{2,1,0:T(1,128)} %bitcast.31, f32[56,1,128]{2,1,0:T(1,128)} %bitcast.32, f32[56,1,128]{2,1,0:T(1,128)} %bitcast.33), custom_call_target="tpu_custom_call" | custom-call | tf_op jit(solution)/shard_map/pallas_call | solution.py:129
  2.1 2.6 %collective-permute-start.4 = (f32[168,128]{1,0:T(8,128)S(1)}, f32[168,128]{1,0:T(8,128)S(1)}, u32[]{:S(2)}, u32[]{:S(2)}) collective-permute-start(f32[168,128]{1,0:T(8,128)S(1)} %bitcast.22), channel_id=1, source_target_pairs={{0,16},{1,3},{2,18},{3,1},{16,0},{17,19},{18,2},{19,17},{4,20},{5,... | collective-permute-start | bytes 258056 | tf_op jit(solution)/shard_map/ppermute | solution.py:18
  4.7 0.0 collective-permute-done.theirs
  4.7 0.1 shard_map.85
  4.8 1.4 %collective-permute-start.1 = (f32[112,128]{1,0:T(8,128)S(1)}, f32[112,128]{1,0:T(8,128)S(1)}, u32[]{:S(2)}, u32[]{:S(2)}) collective-permute-start(f32[112,128]{1,0:T(8,128)S(1)} %get-tuple-element.18), channel_id=1, source_target_pairs={{0,19},{1,18},{2,17},{3,16},{16,3},{17,2},{18,1},{19,0},{4,23},{5,... | collective-permute-start | bytes 172040 | tf_op jit(solution)/shard_map/ppermute | solution.py:18
  6.2 1.4 %collective-permute-start.2 = (f32[112,128]{1,0:T(8,128)S(1)}, f32[112,128]{1,0:T(8,128)S(1)}, u32[]{:S(2)}, u32[]{:S(2)}) collective-permute-start(f32[112,128]{1,0:T(8,128)S(1)} %get-tuple-element.19), channel_id=1, source_target_pairs={{0,17},{1,2},{2,19},{3,0},{16,1},{17,18},{18,3},{19,16},{4,21},{5,... | collective-permute-start | bytes 172040 | tf_op jit(solution)/shard_map/ppermute | solution.py:18
  7.5 0.4 %collective-permute-start.3 = (f32[112,128]{1,0:T(8,128)S(1)}, f32[112,128]{1,0:T(8,128)S(1)}, u32[]{:S(2)}, u32[]{:S(2)}) collective-permute-start(f32[112,128]{1,0:T(8,128)S(1)} %get-tuple-element.20), channel_id=1, source_target_pairs={{0,3},{1,16},{2,1},{3,18},{16,19},{17,0},{18,17},{19,2},{4,7},{5,2... | collective-permute-start | bytes 172040 | tf_op jit(solution)/shard_map/ppermute | solution.py:18
  8.6 0.0 collective-permute-done.4.theirs_state
  8.6 1.1 %collective-permute-done.1.cross = f32[112,128]{1,0:T(8,128)S(1)} collective-permute-done((f32[112,128]{1,0:T(8,128)S(1)}, f32[112,128]{1,0:T(8,128)S(1)}, u32[]{:S(2)}, u32[]{:S(2)}) %collective-permute-start.1) | collective-permute-done | bytes 57376 | tf_op jit(solution)/shard_map/ppermute | solution.py:18
  9.7 0.7 %collective-permute-done.2.near = f32[112,128]{1,0:T(8,128)S(1)} collective-permute-done((f32[112,128]{1,0:T(8,128)S(1)}, f32[112,128]{1,0:T(8,128)S(1)}, u32[]{:S(2)}, u32[]{:S(2)}) %collective-permute-start.2) | collective-permute-done | bytes 57376 | tf_op jit(solution)/shard_map/ppermute | solution.py:18
  10.4 0.8 %collective-permute-done.3.level = f32[112,128]{1,0:T(8,128)S(1)} collective-permute-done((f32[112,128]{1,0:T(8,128)S(1)}, f32[112,128]{1,0:T(8,128)S(1)}, u32[]{:S(2)}, u32[]{:S(2)}) %collective-permute-start.3) | collective-permute-done | bytes 57376 | tf_op jit(solution)/shard_map/ppermute | solution.py:18
  11.2 0.1 shard_map.87.refs_3_
  11.3 1.0 %collective-permute-start.5 = (bf16[112,128]{1,0:T(8,128)(2,1)S(1)}, bf16[112,128]{1,0:T(8,128)(2,1)S(1)}, u32[]{:S(2)}, u32[]{:S(2)}) collective-permute-start(bf16[112,128]{1,0:T(8,128)(2,1)S(1)} %shard_map.87.refs_3_), channel_id=1, source_target_pairs={{0,2},{1,17},{2,0},{3,19},{16,18},{17,1},{18,16},{19,3},{4,6},{5,2... | collective-permute-start | bytes 86024 | tf_op jit(solution)/shard_map/ppermute | solution.py:18
  12.3 0.6 %collective-permute-start.6 = (bf16[112,128]{1,0:T(8,128)(2,1)S(1)}, bf16[112,128]{1,0:T(8,128)(2,1)S(1)}, u32[]{:S(2)}, u32[]{:S(2)}) collective-permute-start(bf16[112,128]{1,0:T(8,128)(2,1)S(1)} %shard_map.87.refs_3_), channel_id=1, source_target_pairs={{0,3},{1,16},{2,1},{3,18},{16,19},{17,0},{18,17},{19,2},{4,7},{5,2... | collective-permute-start | bytes 86024 | tf_op jit(solution)/shard_map/ppermute | solution.py:18
  12.9 0.7 %collective-permute-start.7 = (bf16[112,128]{1,0:T(8,128)(2,1)S(1)}, bf16[112,128]{1,0:T(8,128)(2,1)S(1)}, u32[]{:S(2)}, u32[]{:S(2)}) collective-permute-start(bf16[112,128]{1,0:T(8,128)(2,1)S(1)} %shard_map.87.refs_3_), channel_id=1, source_target_pairs={{0,1},{1,0},{2,3},{3,2},{16,17},{17,16},{18,19},{19,18},{4,5},{5,4... | collective-permute-start | bytes 86024 | tf_op jit(solution)/shard_map/ppermute | solution.py:18
  13.6 0.7 %shard_map.86 = (f32[56,128]{1,0:T(8,128)}, f32[56,128]{1,0:T(8,128)}, f32[56,128]{1,0:T(8,128)}) custom-call(s32[1]{0:T(128)S(6)} %copy.9.step_ref, f32[112,128]{1,0:T(8,128)S(1)} %collective-permute-done.1.cross, f32[112,128]{1,0:T(8,128)S(1)} %collective-permute-done.2.near, f32[112,128]{1,0:T(8,128)S(1)} %collective-permute-done.3.level, ...), custom_call_target="tpu_custom_call" | custom-call | tf_op jit(solution)/shard_map/pallas_call | solution.py:129
  14.2 1.0 %collective-permute-done.5.refs_0_ = bf16[112,128]{1,0:T(8,128)(2,1)S(1)} collective-permute-done((bf16[112,128]{1,0:T(8,128)(2,1)S(1)}, bf16[112,128]{1,0:T(8,128)(2,1)S(1)}, u32[]{:S(2)}, u32[]{:S(2)}) %collective-permute-start.5) | collective-permute-done | bytes 28704 | tf_op jit(solution)/shard_map/ppermute | solution.py:18
  15.2 0.4 %collective-permute-done.6.refs_1_ = bf16[112,128]{1,0:T(8,128)(2,1)S(1)} collective-permute-done((bf16[112,128]{1,0:T(8,128)(2,1)S(1)}, bf16[112,128]{1,0:T(8,128)(2,1)S(1)}, u32[]{:S(2)}, u32[]{:S(2)}) %collective-permute-start.6) | collective-permute-done | bytes 28704 | tf_op jit(solution)/shard_map/ppermute | solution.py:18
  15.6 0.0 collective-permute-done.7.refs_2_
  15.6 0.7 %shard_map.88 = bf16[448,128]{1,0:T(8,128)(2,1)} custom-call(bf16[112,128]{1,0:T(8,128)(2,1)S(1)} %collective-permute-done.5.refs_0_, bf16[112,128]{1,0:T(8,128)(2,1)S(1)} %collective-permute-done.6.refs_1_, bf16[112,128]{1,0:T(8,128)(2,1)S(1)} %collective-permute-done.7.refs_2_, bf16[112,128]{1,0:T(8,128)(2,1)S(1)} %shard_map.87.refs_3_), custom_call_target="tpu_custom_call" | custom-call | tf_op jit(solution)/shard_map/pallas_call | solution.py:129
Async XLA Ops:
  0.6 4.1 %collective-permute-start = (f32[448,128]{1,0:T(8,128)}, f32[448,128]{1,0:T(8,128)S(1)}, u32[]{:S(2)}, u32[]{:S(2)}) collective-permute-start(f32[448,128]{1,0:T(8,128)} %bitcast.28), channel_id=1, source_target_pairs={{0,1},{1,0},{2,3},{3,2},{16,17},{17,16},{18,19},{19,18},{4,5},{5,4... | collective-permute-start | bytes 688136 | tf_op jit(solution)/shard_map/ppermute | solution.py:18
  2.1 6.4 %collective-permute-start.4 = (f32[168,128]{1,0:T(8,128)S(1)}, f32[168,128]{1,0:T(8,128)S(1)}, u32[]{:S(2)}, u32[]{:S(2)}) collective-permute-start(f32[168,128]{1,0:T(8,128)S(1)} %bitcast.22), channel_id=1, source_target_pairs={{0,16},{1,3},{2,18},{3,1},{16,0},{17,19},{18,2},{19,17},{4,20},{5,... | collective-permute-start | bytes 258056 | tf_op jit(solution)/shard_map/ppermute | solution.py:18
  4.8 4.9 %collective-permute-start.1 = (f32[112,128]{1,0:T(8,128)S(1)}, f32[112,128]{1,0:T(8,128)S(1)}, u32[]{:S(2)}, u32[]{:S(2)}) collective-permute-start(f32[112,128]{1,0:T(8,128)S(1)} %get-tuple-element.18), channel_id=1, source_target_pairs={{0,19},{1,18},{2,17},{3,16},{16,3},{17,2},{18,1},{19,0},{4,23},{5,... | collective-permute-start | bytes 172040 | tf_op jit(solution)/shard_map/ppermute | solution.py:18
  6.2 4.2 %collective-permute-start.2 = (f32[112,128]{1,0:T(8,128)S(1)}, f32[112,128]{1,0:T(8,128)S(1)}, u32[]{:S(2)}, u32[]{:S(2)}) collective-permute-start(f32[112,128]{1,0:T(8,128)S(1)} %get-tuple-element.19), channel_id=1, source_target_pairs={{0,17},{1,2},{2,19},{3,0},{16,1},{17,18},{18,3},{19,16},{4,21},{5,... | collective-permute-start | bytes 172040 | tf_op jit(solution)/shard_map/ppermute | solution.py:18
  7.5 3.7 %collective-permute-start.3 = (f32[112,128]{1,0:T(8,128)S(1)}, f32[112,128]{1,0:T(8,128)S(1)}, u32[]{:S(2)}, u32[]{:S(2)}) collective-permute-start(f32[112,128]{1,0:T(8,128)S(1)} %get-tuple-element.20), channel_id=1, source_target_pairs={{0,3},{1,16},{2,1},{3,18},{16,19},{17,0},{18,17},{19,2},{4,7},{5,2... | collective-permute-start | bytes 172040 | tf_op jit(solution)/shard_map/ppermute | solution.py:18
  11.3 3.9 %collective-permute-start.5 = (bf16[112,128]{1,0:T(8,128)(2,1)S(1)}, bf16[112,128]{1,0:T(8,128)(2,1)S(1)}, u32[]{:S(2)}, u32[]{:S(2)}) collective-permute-start(bf16[112,128]{1,0:T(8,128)(2,1)S(1)} %shard_map.87.refs_3_), channel_id=1, source_target_pairs={{0,2},{1,17},{2,0},{3,19},{16,18},{17,1},{18,16},{19,3},{4,6},{5,2... | collective-permute-start | bytes 86024 | tf_op jit(solution)/shard_map/ppermute | solution.py:18
  12.3 3.3 %collective-permute-start.6 = (bf16[112,128]{1,0:T(8,128)(2,1)S(1)}, bf16[112,128]{1,0:T(8,128)(2,1)S(1)}, u32[]{:S(2)}, u32[]{:S(2)}) collective-permute-start(bf16[112,128]{1,0:T(8,128)(2,1)S(1)} %shard_map.87.refs_3_), channel_id=1, source_target_pairs={{0,3},{1,16},{2,1},{3,18},{16,19},{17,0},{18,17},{19,2},{4,7},{5,2... | collective-permute-start | bytes 86024 | tf_op jit(solution)/shard_map/ppermute | solution.py:18
  12.9 2.7 %collective-permute-start.7 = (bf16[112,128]{1,0:T(8,128)(2,1)S(1)}, bf16[112,128]{1,0:T(8,128)(2,1)S(1)}, u32[]{:S(2)}, u32[]{:S(2)}) collective-permute-start(bf16[112,128]{1,0:T(8,128)(2,1)S(1)} %shard_map.87.refs_3_), channel_id=1, source_target_pairs={{0,1},{1,0},{2,3},{3,2},{16,17},{17,16},{18,19},{19,18},{4,5},{5,4... | collective-permute-start | bytes 86024 | tf_op jit(solution)/shard_map/ppermute | solution.py:18

commit v5 on v4

--- a/solution.py
+++ b/solution.py
@@ -107,8 +107,8 @@
     pair, shard = lax.axis_index("pair"), lax.axis_index("dp")
     core, near = shard & 1, (shard >> 1) & 1
     sources = (
+        (pair ^ (1 - core), near ^ core, core ^ 1),
         (pair ^ core, near ^ (1 - core), core),
-        (pair ^ (1 - core), near ^ core, core ^ 1),
         (pair, near, core ^ 1),
         (pair, near, core),
     )
@@ -181,7 +181,7 @@
     news = call(
         functools.partial(own_kernel, size), (row, row, row), step, *sums, state)
 
-    pieces = [send(params, 2, shards), send(params, 3, shards | 1), send(params, 1), params]
+    pieces = [send(params, 3, shards | 1), send(params, 2, shards), send(params, 1), params]
     block, sub = 8 * own, min(8, 8 * own)
     params = call(
         functools.partial(order_kernel, own, tiles), shaped((block * tiles, LANES), jnp.bfloat16),

time: 16.5 us -> 16.8 us (1.018)
  waiting for transfers between devices: 3.95 us -> 4.59 us
  starting transfers between devices: 8.56 us -> 8.16 us
    ppermute x8, waiting for transfers between devices: 3.95 us -> 4.59 us  [send(): lax.ppermute(array, GROUP, [(i, i ^ flip[i & 1]) for i in range(size)])]
    ppermute x8, starting transfers between devices: 8.56 us -> 8.16 us  [send(): lax.ppermute(array, GROUP, [(i, i ^ flip[i & 1]) for i in range(size)])]
where the time goes in v5:
time: 16.8 us; the launch traced here: 16.6 us
  starting transfers between devices  8.16 us (49%)
  waiting for transfers between devices  4.59 us (27%)
  Pallas kernels  2.49 us (15%)
  between operations  1.32 us (8%)
    ppermute x8, starting transfers between devices, send(): lax.ppermute(array, GROUP, [(i, i ^ flip[i & 1]) for i in range(size)])  8.16 us
    ppermute x8, waiting for transfers between devices, send(): lax.ppermute(array, GROUP, [(i, i ^ flip[i & 1]) for i in range(size)])  4.59 us
    pallas_call x5, Pallas kernels, call(): pl.pallas_call(body, out_shape=outs, in_specs=specs, out_specs=jax.tree.m...  2.49 us
  transfers between devices with their start and end apart: 8, of which 5 were waited for; matrix products, arithmetic and copies ran while one was open for 0% of the time, Pallas kernels for 10%

profile of v5, /device:TPU:0, one launch (start us, length us, event | category | flops | bytes accessed | tf_op | source)
XLA Modules:
  0.0 16.6 jit_solution(3120518394596483968)
XLA Ops:
  0.6 0.5 %collective-permute-start = (f32[448,128]{1,0:T(8,128)}, f32[448,128]{1,0:T(8,128)S(1)}, u32[]{:S(2)}, u32[]{:S(2)}) collective-permute-start(f32[448,128]{1,0:T(8,128)} %bitcast.28), channel_id=1, source_target_pairs={{0,1},{1,0},{2,3},{3,2},{16,17},{17,16},{18,19},{19,18},{4,5},{5,4... | collective-permute-start | bytes 688136 | tf_op jit(solution)/shard_map/ppermute | solution.py:18
  1.1 1.0 %shard_map.84 = (f32[112,1,128]{2,1,0:T(1,128)S(1)}, f32[112,1,128]{2,1,0:T(1,128)S(1)}, f32[112,1,128]{2,1,0:T(1,128)S(1)}, f32[168,1,128]{2,1,0:T(1,128)S(1)}) custom-call(f32[56,8,1,128]{3,2,1,0:T(1,128)} %bitcast.29, f32[56,1,128]{2,1,0:T(1,128)} %bitcast.31, f32[56,1,128]{2,1,0:T(1,128)} %bitcast.32, f32[56,1,128]{2,1,0:T(1,128)} %bitcast.33), custom_call_target="tpu_custom_call" | custom-call | tf_op jit(solution)/shard_map/pallas_call | solution.py:129
  2.1 2.6 %collective-permute-start.4 = (f32[168,128]{1,0:T(8,128)S(1)}, f32[168,128]{1,0:T(8,128)S(1)}, u32[]{:S(2)}, u32[]{:S(2)}) collective-permute-start(f32[168,128]{1,0:T(8,128)S(1)} %bitcast.22), channel_id=1, source_target_pairs={{0,16},{1,3},{2,18},{3,1},{16,0},{17,19},{18,2},{19,17},{4,20},{5,... | collective-permute-start | bytes 258056 | tf_op jit(solution)/shard_map/ppermute | solution.py:18
  4.7 0.0 collective-permute-done.theirs
  4.7 0.1 shard_map.85
  4.8 1.4 %collective-permute-start.1 = (f32[112,128]{1,0:T(8,128)S(1)}, f32[112,128]{1,0:T(8,128)S(1)}, u32[]{:S(2)}, u32[]{:S(2)}) collective-permute-start(f32[112,128]{1,0:T(8,128)S(1)} %get-tuple-element.18), channel_id=1, source_target_pairs={{0,19},{1,18},{2,17},{3,16},{16,3},{17,2},{18,1},{19,0},{4,23},{5,... | collective-permute-start | bytes 172040 | tf_op jit(solution)/shard_map/ppermute | solution.py:18
  6.2 1.4 %collective-permute-start.2 = (f32[112,128]{1,0:T(8,128)S(1)}, f32[112,128]{1,0:T(8,128)S(1)}, u32[]{:S(2)}, u32[]{:S(2)}) collective-permute-start(f32[112,128]{1,0:T(8,128)S(1)} %get-tuple-element.19), channel_id=1, source_target_pairs={{0,17},{1,2},{2,19},{3,0},{16,1},{17,18},{18,3},{19,16},{4,21},{5,... | collective-permute-start | bytes 172040 | tf_op jit(solution)/shard_map/ppermute | solution.py:18
  7.5 0.4 %collective-permute-start.3 = (f32[112,128]{1,0:T(8,128)S(1)}, f32[112,128]{1,0:T(8,128)S(1)}, u32[]{:S(2)}, u32[]{:S(2)}) collective-permute-start(f32[112,128]{1,0:T(8,128)S(1)} %get-tuple-element.20), channel_id=1, source_target_pairs={{0,3},{1,16},{2,1},{3,18},{16,19},{17,0},{18,17},{19,2},{4,7},{5,2... | collective-permute-start | bytes 172040 | tf_op jit(solution)/shard_map/ppermute | solution.py:18
  8.6 0.0 collective-permute-done.4.theirs_state
  8.6 1.1 %collective-permute-done.1.cross = f32[112,128]{1,0:T(8,128)S(1)} collective-permute-done((f32[112,128]{1,0:T(8,128)S(1)}, f32[112,128]{1,0:T(8,128)S(1)}, u32[]{:S(2)}, u32[]{:S(2)}) %collective-permute-start.1) | collective-permute-done | bytes 57376 | tf_op jit(solution)/shard_map/ppermute | solution.py:18
  9.7 0.7 %collective-permute-done.2.near = f32[112,128]{1,0:T(8,128)S(1)} collective-permute-done((f32[112,128]{1,0:T(8,128)S(1)}, f32[112,128]{1,0:T(8,128)S(1)}, u32[]{:S(2)}, u32[]{:S(2)}) %collective-permute-start.2) | collective-permute-done | bytes 57376 | tf_op jit(solution)/shard_map/ppermute | solution.py:18
  10.4 0.8 %collective-permute-done.3.level = f32[112,128]{1,0:T(8,128)S(1)} collective-permute-done((f32[112,128]{1,0:T(8,128)S(1)}, f32[112,128]{1,0:T(8,128)S(1)}, u32[]{:S(2)}, u32[]{:S(2)}) %collective-permute-start.3) | collective-permute-done | bytes 57376 | tf_op jit(solution)/shard_map/ppermute | solution.py:18
  11.2 0.1 shard_map.87.refs_3_
  11.3 0.7 %collective-permute-start.5 = (bf16[112,128]{1,0:T(8,128)(2,1)S(1)}, bf16[112,128]{1,0:T(8,128)(2,1)S(1)}, u32[]{:S(2)}, u32[]{:S(2)}) collective-permute-start(bf16[112,128]{1,0:T(8,128)(2,1)S(1)} %shard_map.87.refs_3_), channel_id=1, source_target_pairs={{0,3},{1,16},{2,1},{3,18},{16,19},{17,0},{18,17},{19,2},{4,7},{5,2... | collective-permute-start | bytes 86024 | tf_op jit(solution)/shard_map/ppermute | solution.py:18
  11.9 1.2 %collective-permute-start.6 = (bf16[112,128]{1,0:T(8,128)(2,1)S(1)}, bf16[112,128]{1,0:T(8,128)(2,1)S(1)}, u32[]{:S(2)}, u32[]{:S(2)}) collective-permute-start(bf16[112,128]{1,0:T(8,128)(2,1)S(1)} %shard_map.87.refs_3_), channel_id=1, source_target_pairs={{0,2},{1,17},{2,0},{3,19},{16,18},{17,1},{18,16},{19,3},{4,6},{5,2... | collective-permute-start | bytes 86024 | tf_op jit(solution)/shard_map/ppermute | solution.py:18
  13.1 0.1 collective-permute-start.7
  13.2 0.7 %shard_map.86 = (f32[56,128]{1,0:T(8,128)}, f32[56,128]{1,0:T(8,128)}, f32[56,128]{1,0:T(8,128)}) custom-call(s32[1]{0:T(128)S(6)} %copy.9.step_ref, f32[112,128]{1,0:T(8,128)S(1)} %collective-permute-done.1.cross, f32[112,128]{1,0:T(8,128)S(1)} %collective-permute-done.2.near, f32[112,128]{1,0:T(8,128)S(1)} %collective-permute-done.3.level, ...), custom_call_target="tpu_custom_call" | custom-call | tf_op jit(solution)/shard_map/pallas_call | solution.py:129
  13.8 0.8 %collective-permute-done.5.refs_0_ = bf16[112,128]{1,0:T(8,128)(2,1)S(1)} collective-permute-done((bf16[112,128]{1,0:T(8,128)(2,1)S(1)}, bf16[112,128]{1,0:T(8,128)(2,1)S(1)}, u32[]{:S(2)}, u32[]{:S(2)}) %collective-permute-start.5) | collective-permute-done | bytes 28704 | tf_op jit(solution)/shard_map/ppermute | solution.py:18
  14.6 1.2 %collective-permute-done.6.refs_1_ = bf16[112,128]{1,0:T(8,128)(2,1)S(1)} collective-permute-done((bf16[112,128]{1,0:T(8,128)(2,1)S(1)}, bf16[112,128]{1,0:T(8,128)(2,1)S(1)}, u32[]{:S(2)}, u32[]{:S(2)}) %collective-permute-start.6) | collective-permute-done | bytes 28704 | tf_op jit(solution)/shard_map/ppermute | solution.py:18
  15.8 0.0 collective-permute-done.7.refs_2_
  15.8 0.7 %shard_map.88 = bf16[448,128]{1,0:T(8,128)(2,1)} custom-call(bf16[112,128]{1,0:T(8,128)(2,1)S(1)} %collective-permute-done.5.refs_0_, bf16[112,128]{1,0:T(8,128)(2,1)S(1)} %collective-permute-done.6.refs_1_, bf16[112,128]{1,0:T(8,128)(2,1)S(1)} %collective-permute-done.7.refs_2_, bf16[112,128]{1,0:T(8,128)(2,1)S(1)} %shard_map.87.refs_3_), custom_call_target="tpu_custom_call" | custom-call | tf_op jit(solution)/shard_map/pallas_call | solution.py:129
Async XLA Ops:
  0.6 4.1 %collective-permute-start = (f32[448,128]{1,0:T(8,128)}, f32[448,128]{1,0:T(8,128)S(1)}, u32[]{:S(2)}, u32[]{:S(2)}) collective-permute-start(f32[448,128]{1,0:T(8,128)} %bitcast.28), channel_id=1, source_target_pairs={{0,1},{1,0},{2,3},{3,2},{16,17},{17,16},{18,19},{19,18},{4,5},{5,4... | collective-permute-start | bytes 688136 | tf_op jit(solution)/shard_map/ppermute | solution.py:18
  2.1 6.4 %collective-permute-start.4 = (f32[168,128]{1,0:T(8,128)S(1)}, f32[168,128]{1,0:T(8,128)S(1)}, u32[]{:S(2)}, u32[]{:S(2)}) collective-permute-start(f32[168,128]{1,0:T(8,128)S(1)} %bitcast.22), channel_id=1, source_target_pairs={{0,16},{1,3},{2,18},{3,1},{16,0},{17,19},{18,2},{19,17},{4,20},{5,... | collective-permute-start | bytes 258056 | tf_op jit(solution)/shard_map/ppermute | solution.py:18
  4.8 4.9 %collective-permute-start.1 = (f32[112,128]{1,0:T(8,128)S(1)}, f32[112,128]{1,0:T(8,128)S(1)}, u32[]{:S(2)}, u32[]{:S(2)}) collective-permute-start(f32[112,128]{1,0:T(8,128)S(1)} %get-tuple-element.18), channel_id=1, source_target_pairs={{0,19},{1,18},{2,17},{3,16},{16,3},{17,2},{18,1},{19,0},{4,23},{5,... | collective-permute-start | bytes 172040 | tf_op jit(solution)/shard_map/ppermute | solution.py:18
  6.2 4.2 %collective-permute-start.2 = (f32[112,128]{1,0:T(8,128)S(1)}, f32[112,128]{1,0:T(8,128)S(1)}, u32[]{:S(2)}, u32[]{:S(2)}) collective-permute-start(f32[112,128]{1,0:T(8,128)S(1)} %get-tuple-element.19), channel_id=1, source_target_pairs={{0,17},{1,2},{2,19},{3,0},{16,1},{17,18},{18,3},{19,16},{4,21},{5,... | collective-permute-start | bytes 172040 | tf_op jit(solution)/shard_map/ppermute | solution.py:18
  7.5 3.7 %collective-permute-start.3 = (f32[112,128]{1,0:T(8,128)S(1)}, f32[112,128]{1,0:T(8,128)S(1)}, u32[]{:S(2)}, u32[]{:S(2)}) collective-permute-start(f32[112,128]{1,0:T(8,128)S(1)} %get-tuple-element.20), channel_id=1, source_target_pairs={{0,3},{1,16},{2,1},{3,18},{16,19},{17,0},{18,17},{19,2},{4,7},{5,2... | collective-permute-start | bytes 172040 | tf_op jit(solution)/shard_map/ppermute | solution.py:18
  11.3 3.3 %collective-permute-start.5 = (bf16[112,128]{1,0:T(8,128)(2,1)S(1)}, bf16[112,128]{1,0:T(8,128)(2,1)S(1)}, u32[]{:S(2)}, u32[]{:S(2)}) collective-permute-start(bf16[112,128]{1,0:T(8,128)(2,1)S(1)} %shard_map.87.refs_3_), channel_id=1, source_target_pairs={{0,3},{1,16},{2,1},{3,18},{16,19},{17,0},{18,17},{19,2},{4,7},{5,2... | collective-permute-start | bytes 86024 | tf_op jit(solution)/shard_map/ppermute | solution.py:18
  11.9 3.9 %collective-permute-start.6 = (bf16[112,128]{1,0:T(8,128)(2,1)S(1)}, bf16[112,128]{1,0:T(8,128)(2,1)S(1)}, u32[]{:S(2)}, u32[]{:S(2)}) collective-permute-start(bf16[112,128]{1,0:T(8,128)(2,1)S(1)} %shard_map.87.refs_3_), channel_id=1, source_target_pairs={{0,2},{1,17},{2,0},{3,19},{16,18},{17,1},{18,16},{19,3},{4,6},{5,2... | collective-permute-start | bytes 86024 | tf_op jit(solution)/shard_map/ppermute | solution.py:18
  13.1 2.7 %collective-permute-start.7 = (bf16[112,128]{1,0:T(8,128)(2,1)S(1)}, bf16[112,128]{1,0:T(8,128)(2,1)S(1)}, u32[]{:S(2)}, u32[]{:S(2)}) collective-permute-start(bf16[112,128]{1,0:T(8,128)(2,1)S(1)} %shard_map.87.refs_3_), channel_id=1, source_target_pairs={{0,1},{1,0},{2,3},{3,2},{16,17},{17,16},{18,19},{19,18},{4,5},{5,4... | collective-permute-start | bytes 86024 | tf_op jit(solution)/shard_map/ppermute | solution.py:18

commit v6 on v3

--- a/solution.py
+++ b/solution.py
@@ -57,7 +57,7 @@
         copy.wait()
 
 
-def sum_kernel(dims, theirs, own_keep, own_give, cross_ref, near_ref, level_ref, keep_ref):
+def sum_kernel(dims, theirs, own_keep, own_give, state, level_ref, cross_ref, near_ref, keep_ref):
     tiles, rows = dims[2], 2 * dims[0] * dims[1]
     for to, (kept, given) in my_rows(*dims):
         keep = own_keep[to, :] + theirs[row_at(kept, tiles, rows), :]
@@ -66,6 +66,7 @@
         give = own_give[to, :] + theirs[row_at(given, tiles, rows), :]
         cross_ref[to, :] = give
         near_ref[to, :] = give
+    level_ref[keep_ref.shape[0]:, :] = state[...]
 
 
 def adam(total, master, moment, second, count):
@@ -78,7 +79,7 @@
 
 
 def totals(size, sums):
-    cross, near, level, keep = (s[...] for s in sums)
+    level, cross, near, keep = (s[:2 * size] for s in sums)
     flip = lambda rows: (rows[size:], rows[:size])
     return [
         (c + n) + (l + k)
@@ -90,17 +91,17 @@
     return [ref[i * size:(i + 1) * size, :] for i in range(3)]
 
 
-def params_kernel(size, step_ref, cross, near, level, keep, state, theirs_state, out_ref):
+def params_kernel(size, step_ref, level, cross, near, keep, state, out_ref):
     count = jnp.full((1, LANES), step_ref[0], jnp.int32).astype(jnp.float32)
-    mine, theirs = totals(size, (cross, near, level, keep))
+    mine, theirs = totals(size, (level, cross, near, keep))
     a, _, _ = adam(mine, *thirds(size, state), count)
-    b, _, _ = adam(theirs, *thirds(size, theirs_state), count)
+    b, _, _ = adam(theirs, *thirds(size, level.at[pl.ds(2 * size, 3 * size)]), count)
     out_ref[...] = jnp.concatenate([a, b], axis=0).astype(out_ref.dtype)
 
 
-def own_kernel(size, step_ref, cross, near, level, keep, state, m_ref, v_ref, s_ref):
+def own_kernel(size, step_ref, level, cross, near, keep, state, m_ref, v_ref, s_ref):
     count = jnp.full((1, LANES), step_ref[0], jnp.int32).astype(jnp.float32)
-    mine, _ = totals(size, (cross, near, level, keep))
+    mine, _ = totals(size, (level, cross, near, keep))
     m_ref[...], v_ref[...], s_ref[...] = adam(mine, *thirds(size, state), count)
 
 
@@ -161,8 +162,9 @@
         functools.partial(front_kernel, dims), (picked, picked, shaped((3 * size, 1, LANES), f32)),
         *(pltpu.with_memory_space_constraint(a, pltpu.HBM) for a in (blocks, *flat)), hbm=True,
         scratch=[pltpu.SemaphoreType.DMA((3 + 2 * (half.shape[0] // tiles),))]))
-    theirs_state = send(state, shards, 2)
-    to_cross, to_near, to_level, keep = call(functools.partial(sum_kernel, dims), (half, half, half, half), theirs, keep, give)
+    joined = shaped((half.shape[0] + 3 * size, LANES), f32)
+    to_level, to_cross, to_near, keep = call(
+        functools.partial(sum_kernel, dims), (joined, half, half, half), theirs, keep, give, state)
 
     for bit in reversed(far):
         low = (shard & bit) == 0
@@ -170,14 +172,14 @@
         mine = jnp.where(low, held[:, :, 0], held[:, :, 1])
         other = jnp.where(low, held[:, :, 1], held[:, :, 0])
         keep, to_near = (mine + send(other, bit)).reshape(2, -1, LANES)
-        to_cross, to_level = to_near, keep
-
-    cross, near, level = send(to_cross, shards | 2), send(to_near, 2, shards), send(to_level, shards, 2)
-    sums = (cross, near, level, keep)
+        to_cross, to_level = to_near, jnp.concatenate([keep, state], axis=0)
+
+    level, cross, near = send(to_level, shards, 2), send(to_cross, shards | 2), send(to_near, 2, shards)
+    sums = (level, cross, near, keep)
 
     params = call(
         functools.partial(params_kernel, size), shaped((2 * size, LANES), jnp.bfloat16),
-        step, *sums, state, theirs_state)
+        step, *sums, state)
     row = shaped((size, LANES), f32)
     news = call(
         functools.partial(own_kernel, size), (row, row, row), step, *sums, state)

time: 16.3 us -> 16.8 us (1.031)
  waiting for transfers between devices: 3.78 us -> 5.96 us
  starting transfers between devices: 8.59 us -> 6.94 us
    ppermute x8 -> x7, waiting for transfers between devices: 3.78 us -> 5.96 us  [send(): lax.ppermute(array, GROUP, [(i, i ^ flip[i & 1]) for i in range(size)])]
    ppermute x8 -> x7, starting transfers between devices: 8.59 us -> 6.94 us  [send(): lax.ppermute(array, GROUP, [(i, i ^ flip[i & 1]) for i in range(size)])]
  transfers between devices with their start and end apart: 8 -> 7, of which waited for: 5 -> 5; matrix products, arithmetic and copies ran while one was open for 0% -> 0% of each run, Pallas kernels for 10% -> 9%
where the time goes in v6:
time: 16.8 us; the launch traced here: 16.6 us
  starting transfers between devices  6.94 us (41%)
  waiting for transfers between devices  5.96 us (35%)
  Pallas kernels  2.42 us (14%)
  between operations  1.3 us (8%)
    ppermute x7, starting transfers between devices, send(): lax.ppermute(array, GROUP, [(i, i ^ flip[i & 1]) for i in range(size)])  6.94 us
    ppermute x7, waiting for transfers between devices, send(): lax.ppermute(array, GROUP, [(i, i ^ flip[i & 1]) for i in range(size)])  5.96 us
    pallas_call x5, Pallas kernels, call(): pl.pallas_call(body, out_shape=outs, in_specs=specs, out_specs=jax.tree.m...  2.42 us
  transfers between devices with their start and end apart: 7, of which 5 were waited for; matrix products, arithmetic and copies ran while one was open for 0% of the time, Pallas kernels for 9%

profile of v6, /device:TPU:0, one launch (start us, length us, event | category | flops | bytes accessed | tf_op | source)
XLA Modules:
  0.0 16.6 jit_solution(1598641100438226710)
XLA Ops:
  0.6 0.5 %collective-permute-start = (f32[448,128]{1,0:T(8,128)}, f32[448,128]{1,0:T(8,128)S(1)}, u32[]{:S(2)}, u32[]{:S(2)}) collective-permute-start(f32[448,128]{1,0:T(8,128)} %bitcast.26), channel_id=1, source_target_pairs={{0,1},{1,0},{2,3},{3,2},{16,17},{17,16},{18,19},{19,18},{4,5},{5,4... | collective-permute-start | bytes 688136 | tf_op jit(solution)/shard_map/ppermute | solution.py:18
  1.1 0.9 %shard_map.84 = (f32[112,1,128]{2,1,0:T(1,128)S(1)}, f32[112,1,128]{2,1,0:T(1,128)S(1)}, f32[168,1,128]{2,1,0:T(1,128)S(1)}) custom-call(f32[56,8,1,128]{3,2,1,0:T(1,128)} %bitcast.27, f32[56,1,128]{2,1,0:T(1,128)} %bitcast.29, f32[56,1,128]{2,1,0:T(1,128)} %bitcast.30, f32[56,1,128]{2,1,0:T(1,128)} %bitcast.31), custom_call_target="tpu_custom_call" | custom-call | tf_op jit(solution)/shard_map/pallas_call | solution.py:132
  2.1 0.4 %collective-permute-done.theirs = f32[448,128]{1,0:T(8,128)S(1)} collective-permute-done((f32[448,128]{1,0:T(8,128)}, f32[448,128]{1,0:T(8,128)S(1)}, u32[]{:S(2)}, u32[]{:S(2)}) %collective-permute-start) | collective-permute-done | bytes 229408 | tf_op jit(solution)/shard_map/ppermute | solution.py:18
  2.5 3.0 %collective-permute-start.1 = (f32[280,128]{1,0:T(8,128)S(1)}, f32[280,128]{1,0:T(8,128)S(1)}, u32[]{:S(2)}, u32[]{:S(2)}) collective-permute-start(f32[280,128]{1,0:T(8,128)S(1)} %get-tuple-element.17), channel_id=1, source_target_pairs={{0,16},{1,3},{2,18},{3,1},{16,0},{17,19},{18,2},{19,17},{4,20},{5,... | collective-permute-start | bytes 430088 | tf_op jit(solution)/shard_map/ppermute | solution.py:18
  5.5 1.4 %collective-permute-start.2 = (f32[112,128]{1,0:T(8,128)S(1)}, f32[112,128]{1,0:T(8,128)S(1)}, u32[]{:S(2)}, u32[]{:S(2)}) collective-permute-start(f32[112,128]{1,0:T(8,128)S(1)} %get-tuple-element.18), channel_id=1, source_target_pairs={{0,18},{1,19},{2,16},{3,17},{16,2},{17,3},{18,0},{19,1},{4,22},{5,... | collective-permute-start | bytes 172040 | tf_op jit(solution)/shard_map/ppermute | solution.py:18
  6.9 0.1 collective-permute-start.3
  7.7 2.9 %collective-permute-done.2.cross = f32[112,128]{1,0:T(8,128)S(1)} collective-permute-done((f32[112,128]{1,0:T(8,128)S(1)}, f32[112,128]{1,0:T(8,128)S(1)}, u32[]{:S(2)}, u32[]{:S(2)}) %collective-permute-start.2) | collective-permute-done | bytes 57376 | tf_op jit(solution)/shard_map/ppermute | solution.py:18
  10.6 0.5 %collective-permute-done.3.near = f32[112,128]{1,0:T(8,128)S(1)} collective-permute-done((f32[112,128]{1,0:T(8,128)S(1)}, f32[112,128]{1,0:T(8,128)S(1)}, u32[]{:S(2)}, u32[]{:S(2)}) %collective-permute-start.3) | collective-permute-done | bytes 57376 | tf_op jit(solution)/shard_map/ppermute | solution.py:18
  11.1 0.0 collective-permute-done.1.level
  11.1 0.1 shard_map.87.refs_3_
  11.2 0.8 %collective-permute-start.4 = (bf16[112,128]{1,0:T(8,128)(2,1)S(1)}, bf16[112,128]{1,0:T(8,128)(2,1)S(1)}, u32[]{:S(2)}, u32[]{:S(2)}) collective-permute-start(bf16[112,128]{1,0:T(8,128)(2,1)S(1)} %shard_map.87.refs_3_), channel_id=1, source_target_pairs={{0,3},{1,16},{2,1},{3,18},{16,19},{17,0},{18,17},{19,2},{4,7},{5,2... | collective-permute-start | bytes 86024 | tf_op jit(solution)/shard_map/ppermute | solution.py:18
  12.0 0.8 %collective-permute-start.5 = (bf16[112,128]{1,0:T(8,128)(2,1)S(1)}, bf16[112,128]{1,0:T(8,128)(2,1)S(1)}, u32[]{:S(2)}, u32[]{:S(2)}) collective-permute-start(bf16[112,128]{1,0:T(8,128)(2,1)S(1)} %shard_map.87.refs_3_), channel_id=1, source_target_pairs={{0,2},{1,17},{2,0},{3,19},{16,18},{17,1},{18,16},{19,3},{4,6},{5,2... | collective-permute-start | bytes 86024 | tf_op jit(solution)/shard_map/ppermute | solution.py:18
  12.8 0.3 %collective-permute-start.6 = (bf16[112,128]{1,0:T(8,128)(2,1)S(1)}, bf16[112,128]{1,0:T(8,128)(2,1)S(1)}, u32[]{:S(2)}, u32[]{:S(2)}) collective-permute-start(bf16[112,128]{1,0:T(8,128)(2,1)S(1)} %shard_map.87.refs_3_), channel_id=1, source_target_pairs={{0,1},{1,0},{2,3},{3,2},{16,17},{17,16},{18,19},{19,18},{4,5},{5,4... | collective-permute-start | bytes 86024 | tf_op jit(solution)/shard_map/ppermute | solution.py:18
  13.1 0.7 %shard_map.86 = (f32[56,128]{1,0:T(8,128)}, f32[56,128]{1,0:T(8,128)}, f32[56,128]{1,0:T(8,128)}) custom-call(s32[1]{0:T(128)S(6)} %copy.9.step_ref, f32[280,128]{1,0:T(8,128)S(1)} %collective-permute-done.1.level, f32[112,128]{1,0:T(8,128)S(1)} %collective-permute-done.2.cross, f32[112,128]{1,0:T(8,128)S(1)} %collective-permute-done.3.near, ...), custom_call_target="tpu_custom_call" | custom-call | tf_op jit(solution)/shard_map/pallas_call | solution.py:132
  13.7 0.8 %collective-permute-done.4.refs_0_ = bf16[112,128]{1,0:T(8,128)(2,1)S(1)} collective-permute-done((bf16[112,128]{1,0:T(8,128)(2,1)S(1)}, bf16[112,128]{1,0:T(8,128)(2,1)S(1)}, u32[]{:S(2)}, u32[]{:S(2)}) %collective-permute-start.4) | collective-permute-done | bytes 28704 | tf_op jit(solution)/shard_map/ppermute | solution.py:18
  14.5 1.3 %collective-permute-done.5.refs_1_ = bf16[112,128]{1,0:T(8,128)(2,1)S(1)} collective-permute-done((bf16[112,128]{1,0:T(8,128)(2,1)S(1)}, bf16[112,128]{1,0:T(8,128)(2,1)S(1)}, u32[]{:S(2)}, u32[]{:S(2)}) %collective-permute-start.5) | collective-permute-done | bytes 28704 | tf_op jit(solution)/shard_map/ppermute | solution.py:18
  15.9 0.0 collective-permute-done.6.refs_2_
  15.9 0.7 %shard_map.88 = bf16[448,128]{1,0:T(8,128)(2,1)} custom-call(bf16[112,128]{1,0:T(8,128)(2,1)S(1)} %collective-permute-done.4.refs_0_, bf16[112,128]{1,0:T(8,128)(2,1)S(1)} %collective-permute-done.5.refs_1_, bf16[112,128]{1,0:T(8,128)(2,1)S(1)} %collective-permute-done.6.refs_2_, bf16[112,128]{1,0:T(8,128)(2,1)S(1)} %shard_map.87.refs_3_), custom_call_target="tpu_custom_call" | custom-call | tf_op jit(solution)/shard_map/pallas_call | solution.py:132
  (1 shorter events, 0.0 us)
Async XLA Ops:
  0.6 1.8 %collective-permute-start = (f32[448,128]{1,0:T(8,128)}, f32[448,128]{1,0:T(8,128)S(1)}, u32[]{:S(2)}, u32[]{:S(2)}) collective-permute-start(f32[448,128]{1,0:T(8,128)} %bitcast.26), channel_id=1, source_target_pairs={{0,1},{1,0},{2,3},{3,2},{16,17},{17,16},{18,19},{19,18},{4,5},{5,4... | collective-permute-start | bytes 688136 | tf_op jit(solution)/shard_map/ppermute | solution.py:18
  2.5 8.6 %collective-permute-start.1 = (f32[280,128]{1,0:T(8,128)S(1)}, f32[280,128]{1,0:T(8,128)S(1)}, u32[]{:S(2)}, u32[]{:S(2)}) collective-permute-start(f32[280,128]{1,0:T(8,128)S(1)} %get-tuple-element.17), channel_id=1, source_target_pairs={{0,16},{1,3},{2,18},{3,1},{16,0},{17,19},{18,2},{19,17},{4,20},{5,... | collective-permute-start | bytes 430088 | tf_op jit(solution)/shard_map/ppermute | solution.py:18
  5.5 5.1 %collective-permute-start.2 = (f32[112,128]{1,0:T(8,128)S(1)}, f32[112,128]{1,0:T(8,128)S(1)}, u32[]{:S(2)}, u32[]{:S(2)}) collective-permute-start(f32[112,128]{1,0:T(8,128)S(1)} %get-tuple-element.18), channel_id=1, source_target_pairs={{0,18},{1,19},{2,16},{3,17},{16,2},{17,3},{18,0},{19,1},{4,22},{5,... | collective-permute-start | bytes 172040 | tf_op jit(solution)/shard_map/ppermute | solution.py:18
  6.9 4.2 %collective-permute-start.3 = (f32[112,128]{1,0:T(8,128)S(1)}, f32[112,128]{1,0:T(8,128)S(1)}, u32[]{:S(2)}, u32[]{:S(2)}) collective-permute-start(f32[112,128]{1,0:T(8,128)S(1)} %get-tuple-element.19), channel_id=1, source_target_pairs={{0,2},{1,17},{2,0},{3,19},{16,18},{17,1},{18,16},{19,3},{4,6},{5,2... | collective-permute-start | bytes 172040 | tf_op jit(solution)/shard_map/ppermute | solution.py:18
  11.2 3.3 %collective-permute-start.4 = (bf16[112,128]{1,0:T(8,128)(2,1)S(1)}, bf16[112,128]{1,0:T(8,128)(2,1)S(1)}, u32[]{:S(2)}, u32[]{:S(2)}) collective-permute-start(bf16[112,128]{1,0:T(8,128)(2,1)S(1)} %shard_map.87.refs_3_), channel_id=1, source_target_pairs={{0,3},{1,16},{2,1},{3,18},{16,19},{17,0},{18,17},{19,2},{4,7},{5,2... | collective-permute-start | bytes 86024 | tf_op jit(solution)/shard_map/ppermute | solution.py:18
  12.0 3.9 %collective-permute-start.5 = (bf16[112,128]{1,0:T(8,128)(2,1)S(1)}, bf16[112,128]{1,0:T(8,128)(2,1)S(1)}, u32[]{:S(2)}, u32[]{:S(2)}) collective-permute-start(bf16[112,128]{1,0:T(8,128)(2,1)S(1)} %shard_map.87.refs_3_), channel_id=1, source_target_pairs={{0,2},{1,17},{2,0},{3,19},{16,18},{17,1},{18,16},{19,3},{4,6},{5,2... | collective-permute-start | bytes 86024 | tf_op jit(solution)/shard_map/ppermute | solution.py:18
  12.8 3.0 %collective-permute-start.6 = (bf16[112,128]{1,0:T(8,128)(2,1)S(1)}, bf16[112,128]{1,0:T(8,128)(2,1)S(1)}, u32[]{:S(2)}, u32[]{:S(2)}) collective-permute-start(bf16[112,128]{1,0:T(8,128)(2,1)S(1)} %shard_map.87.refs_3_), channel_id=1, source_target_pairs={{0,1},{1,0},{2,3},{3,2},{16,17},{17,16},{18,19},{19,18},{4,5},{5,4... | collective-permute-start | bytes 86024 | tf_op jit(solution)/shard_map/ppermute | solution.py:18

commit v7 on v3

--- a/solution.py
+++ b/solution.py
@@ -78,7 +78,7 @@
 
 
 def totals(size, sums):
-    cross, near, level, keep = (s[...] for s in sums)
+    level, cross, near, keep = (s[...] for s in sums)
     flip = lambda rows: (rows[size:], rows[:size])
     return [
         (c + n) + (l + k)
@@ -90,17 +90,17 @@
     return [ref[i * size:(i + 1) * size, :] for i in range(3)]
 
 
-def params_kernel(size, step_ref, cross, near, level, keep, state, theirs_state, out_ref):
+def params_kernel(size, step_ref, level, cross, near, keep, state, theirs_state, out_ref):
     count = jnp.full((1, LANES), step_ref[0], jnp.int32).astype(jnp.float32)
-    mine, theirs = totals(size, (cross, near, level, keep))
+    mine, theirs = totals(size, (level, cross, near, keep))
     a, _, _ = adam(mine, *thirds(size, state), count)
     b, _, _ = adam(theirs, *thirds(size, theirs_state), count)
     out_ref[...] = jnp.concatenate([a, b], axis=0).astype(out_ref.dtype)
 
 
-def own_kernel(size, step_ref, cross, near, level, keep, state, m_ref, v_ref, s_ref):
+def own_kernel(size, step_ref, level, cross, near, keep, state, m_ref, v_ref, s_ref):
     count = jnp.full((1, LANES), step_ref[0], jnp.int32).astype(jnp.float32)
-    mine, _ = totals(size, (cross, near, level, keep))
+    mine, _ = totals(size, (level, cross, near, keep))
     m_ref[...], v_ref[...], s_ref[...] = adam(mine, *thirds(size, state), count)
 
 
@@ -173,7 +173,7 @@
         to_cross, to_level = to_near, keep
 
     cross, near, level = send(to_cross, shards | 2), send(to_near, 2, shards), send(to_level, shards, 2)
-    sums = (cross, near, level, keep)
+    sums = (level, cross, near, keep)
 
     params = call(
         functools.partial(params_kernel, size), shaped((2 * size, LANES), jnp.bfloat16),

time: 16.3 us -> 17 us (1.043)
  waiting for transfers between devices: 3.78 us -> 4.44 us
    ppermute x8, waiting for transfers between devices: 3.78 us -> 4.44 us  [send(): lax.ppermute(array, GROUP, [(i, i ^ flip[i & 1]) for i in range(size)])]
  transfers between devices with their start and end apart: 8 -> 8, of which waited for: 5 -> 4; matrix products, arithmetic and copies ran while one was open for 0% -> 0% of each run, Pallas kernels for 10% -> 10%
where the time goes in v7:
time: 17 us; the launch traced here: 16.8 us
  starting transfers between devices  8.59 us (51%)
  waiting for transfers between devices  4.44 us (26%)
  Pallas kernels  2.42 us (14%)
  between operations  1.31 us (8%)
    ppermute x8, starting transfers between devices, send(): lax.ppermute(array, GROUP, [(i, i ^ flip[i & 1]) for i in range(size)])  8.59 us
    ppermute x8, waiting for transfers between devices, send(): lax.ppermute(array, GROUP, [(i, i ^ flip[i & 1]) for i in range(size)])  4.44 us
    pallas_call x5, Pallas kernels, call(): pl.pallas_call(body, out_shape=outs, in_specs=specs, out_specs=jax.tree.m...  2.42 us
  transfers between devices with their start and end apart: 8, of which 4 were waited for; matrix products, arithmetic and copies ran while one was open for 0% of the time, Pallas kernels for 10%

profile of v7, /device:TPU:0, one launch (start us, length us, event | category | flops | bytes accessed | tf_op | source)
XLA Modules:
  0.0 16.8 jit_solution(13839542504853351544)
XLA Ops:
  0.6 0.5 %collective-permute-start = (f32[448,128]{1,0:T(8,128)}, f32[448,128]{1,0:T(8,128)S(1)}, u32[]{:S(2)}, u32[]{:S(2)}) collective-permute-start(f32[448,128]{1,0:T(8,128)} %bitcast.26), channel_id=1, source_target_pairs={{0,1},{1,0},{2,3},{3,2},{16,17},{17,16},{18,19},{19,18},{4,5},{5,4... | collective-permute-start | bytes 688136 | tf_op jit(solution)/shard_map/ppermute | solution.py:18
  1.1 0.9 %shard_map.84 = (f32[112,1,128]{2,1,0:T(1,128)S(1)}, f32[112,1,128]{2,1,0:T(1,128)S(1)}, f32[168,1,128]{2,1,0:T(1,128)S(1)}) custom-call(f32[56,8,1,128]{3,2,1,0:T(1,128)} %bitcast.27, f32[56,1,128]{2,1,0:T(1,128)} %bitcast.29, f32[56,1,128]{2,1,0:T(1,128)} %bitcast.30, f32[56,1,128]{2,1,0:T(1,128)} %bitcast.31), custom_call_target="tpu_custom_call" | custom-call | tf_op jit(solution)/shard_map/pallas_call | solution.py:131
  2.1 2.6 %collective-permute-start.4 = (f32[168,128]{1,0:T(8,128)S(1)}, f32[168,128]{1,0:T(8,128)S(1)}, u32[]{:S(2)}, u32[]{:S(2)}) collective-permute-start(f32[168,128]{1,0:T(8,128)S(1)} %bitcast.21), channel_id=1, source_target_pairs={{0,16},{1,3},{2,18},{3,1},{16,0},{17,19},{18,2},{19,17},{4,20},{5,... | collective-permute-start | bytes 258056 | tf_op jit(solution)/shard_map/ppermute | solution.py:18
  4.7 0.0 collective-permute-done.theirs
  4.7 0.8 %collective-permute-start.1 = (f32[112,128]{1,0:T(8,128)S(1)}, f32[112,128]{1,0:T(8,128)S(1)}, u32[]{:S(2)}, u32[]{:S(2)}) collective-permute-start(f32[112,128]{1,0:T(8,128)S(1)} %get-tuple-element.16), channel_id=1, source_target_pairs={{0,16},{1,3},{2,18},{3,1},{16,0},{17,19},{18,2},{19,17},{4,20},{5,... | collective-permute-start | bytes 172040 | tf_op jit(solution)/shard_map/ppermute | solution.py:18
  5.5 2.3 %collective-permute-start.2 = (f32[112,128]{1,0:T(8,128)S(1)}, f32[112,128]{1,0:T(8,128)S(1)}, u32[]{:S(2)}, u32[]{:S(2)}) collective-permute-start(f32[112,128]{1,0:T(8,128)S(1)} %get-tuple-element.17), channel_id=1, source_target_pairs={{0,18},{1,19},{2,16},{3,17},{16,2},{17,3},{18,0},{19,1},{4,22},{5,... | collective-permute-start | bytes 172040 | tf_op jit(solution)/shard_map/ppermute | solution.py:18
  7.7 0.5 %collective-permute-start.3 = (f32[112,128]{1,0:T(8,128)S(1)}, f32[112,128]{1,0:T(8,128)S(1)}, u32[]{:S(2)}, u32[]{:S(2)}) collective-permute-start(f32[112,128]{1,0:T(8,128)S(1)} %get-tuple-element.18), channel_id=1, source_target_pairs={{0,2},{1,17},{2,0},{3,19},{16,18},{17,1},{18,16},{19,3},{4,6},{5,2... | collective-permute-start | bytes 172040 | tf_op jit(solution)/shard_map/ppermute | solution.py:18
  8.9 0.0 collective-permute-done.4.theirs_state
  8.9 0.0 collective-permute-done.1.level
  9.0 1.7 %collective-permute-done.2.cross = f32[112,128]{1,0:T(8,128)S(1)} collective-permute-done((f32[112,128]{1,0:T(8,128)S(1)}, f32[112,128]{1,0:T(8,128)S(1)}, u32[]{:S(2)}, u32[]{:S(2)}) %collective-permute-start.2) | collective-permute-done | bytes 57376 | tf_op jit(solution)/shard_map/ppermute | solution.py:18
  10.6 1.3 %collective-permute-done.3.near = f32[112,128]{1,0:T(8,128)S(1)} collective-permute-done((f32[112,128]{1,0:T(8,128)S(1)}, f32[112,128]{1,0:T(8,128)S(1)}, u32[]{:S(2)}, u32[]{:S(2)}) %collective-permute-start.3) | collective-permute-done | bytes 57376 | tf_op jit(solution)/shard_map/ppermute | solution.py:18
  11.9 0.1 shard_map.87.refs_3_
  12.0 0.2 collective-permute-start.5
  12.1 0.6 %collective-permute-start.6 = (bf16[112,128]{1,0:T(8,128)(2,1)S(1)}, bf16[112,128]{1,0:T(8,128)(2,1)S(1)}, u32[]{:S(2)}, u32[]{:S(2)}) collective-permute-start(bf16[112,128]{1,0:T(8,128)(2,1)S(1)} %shard_map.87.refs_3_), channel_id=1, source_target_pairs={{0,2},{1,17},{2,0},{3,19},{16,18},{17,1},{18,16},{19,3},{4,6},{5,2... | collective-permute-start | bytes 86024 | tf_op jit(solution)/shard_map/ppermute | solution.py:18
  12.7 1.2 %collective-permute-start.7 = (bf16[112,128]{1,0:T(8,128)(2,1)S(1)}, bf16[112,128]{1,0:T(8,128)(2,1)S(1)}, u32[]{:S(2)}, u32[]{:S(2)}) collective-permute-start(bf16[112,128]{1,0:T(8,128)(2,1)S(1)} %shard_map.87.refs_3_), channel_id=1, source_target_pairs={{0,1},{1,0},{2,3},{3,2},{16,17},{17,16},{18,19},{19,18},{4,5},{5,4... | collective-permute-start | bytes 86024 | tf_op jit(solution)/shard_map/ppermute | solution.py:18
  13.9 0.7 %shard_map.86 = (f32[56,128]{1,0:T(8,128)}, f32[56,128]{1,0:T(8,128)}, f32[56,128]{1,0:T(8,128)}) custom-call(s32[1]{0:T(128)S(6)} %copy.9.step_ref, f32[112,128]{1,0:T(8,128)S(1)} %collective-permute-done.1.level, f32[112,128]{1,0:T(8,128)S(1)} %collective-permute-done.2.cross, f32[112,128]{1,0:T(8,128)S(1)} %collective-permute-done.3.near, ...), custom_call_target="tpu_custom_call" | custom-call | tf_op jit(solution)/shard_map/pallas_call | solution.py:131
  14.6 0.8 %collective-permute-done.5.refs_0_ = bf16[112,128]{1,0:T(8,128)(2,1)S(1)} collective-permute-done((bf16[112,128]{1,0:T(8,128)(2,1)S(1)}, bf16[112,128]{1,0:T(8,128)(2,1)S(1)}, u32[]{:S(2)}, u32[]{:S(2)}) %collective-permute-start.5) | collective-permute-done | bytes 28704 | tf_op jit(solution)/shard_map/ppermute | solution.py:18
  15.3 0.7 %collective-permute-done.6.refs_1_ = bf16[112,128]{1,0:T(8,128)(2,1)S(1)} collective-permute-done((bf16[112,128]{1,0:T(8,128)(2,1)S(1)}, bf16[112,128]{1,0:T(8,128)(2,1)S(1)}, u32[]{:S(2)}, u32[]{:S(2)}) %collective-permute-start.6) | collective-permute-done | bytes 28704 | tf_op jit(solution)/shard_map/ppermute | solution.py:18
  16.0 0.0 collective-permute-done.7.refs_2_
  16.0 0.7 %shard_map.88 = bf16[448,128]{1,0:T(8,128)(2,1)} custom-call(bf16[112,128]{1,0:T(8,128)(2,1)S(1)} %collective-permute-done.5.refs_0_, bf16[112,128]{1,0:T(8,128)(2,1)S(1)} %collective-permute-done.6.refs_1_, bf16[112,128]{1,0:T(8,128)(2,1)S(1)} %collective-permute-done.7.refs_2_, bf16[112,128]{1,0:T(8,128)(2,1)S(1)} %shard_map.87.refs_3_), custom_call_target="tpu_custom_call" | custom-call | tf_op jit(solution)/shard_map/pallas_call | solution.py:131
  (1 shorter events, 0.0 us)
Async XLA Ops:
  0.6 4.0 %collective-permute-start = (f32[448,128]{1,0:T(8,128)}, f32[448,128]{1,0:T(8,128)S(1)}, u32[]{:S(2)}, u32[]{:S(2)}) collective-permute-start(f32[448,128]{1,0:T(8,128)} %bitcast.26), channel_id=1, source_target_pairs={{0,1},{1,0},{2,3},{3,2},{16,17},{17,16},{18,19},{19,18},{4,5},{5,4... | collective-permute-start | bytes 688136 | tf_op jit(solution)/shard_map/ppermute | solution.py:18
  2.1 6.9 %collective-permute-start.4 = (f32[168,128]{1,0:T(8,128)S(1)}, f32[168,128]{1,0:T(8,128)S(1)}, u32[]{:S(2)}, u32[]{:S(2)}) collective-permute-start(f32[168,128]{1,0:T(8,128)S(1)} %bitcast.21), channel_id=1, source_target_pairs={{0,16},{1,3},{2,18},{3,1},{16,0},{17,19},{18,2},{19,17},{4,20},{5,... | collective-permute-start | bytes 258056 | tf_op jit(solution)/shard_map/ppermute | solution.py:18
  4.7 4.2 %collective-permute-start.1 = (f32[112,128]{1,0:T(8,128)S(1)}, f32[112,128]{1,0:T(8,128)S(1)}, u32[]{:S(2)}, u32[]{:S(2)}) collective-permute-start(f32[112,128]{1,0:T(8,128)S(1)} %get-tuple-element.16), channel_id=1, source_target_pairs={{0,16},{1,3},{2,18},{3,1},{16,0},{17,19},{18,2},{19,17},{4,20},{5,... | collective-permute-start | bytes 172040 | tf_op jit(solution)/shard_map/ppermute | solution.py:18
  5.5 5.1 %collective-permute-start.2 = (f32[112,128]{1,0:T(8,128)S(1)}, f32[112,128]{1,0:T(8,128)S(1)}, u32[]{:S(2)}, u32[]{:S(2)}) collective-permute-start(f32[112,128]{1,0:T(8,128)S(1)} %get-tuple-element.17), channel_id=1, source_target_pairs={{0,18},{1,19},{2,16},{3,17},{16,2},{17,3},{18,0},{19,1},{4,22},{5,... | collective-permute-start | bytes 172040 | tf_op jit(solution)/shard_map/ppermute | solution.py:18
  7.7 4.2 %collective-permute-start.3 = (f32[112,128]{1,0:T(8,128)S(1)}, f32[112,128]{1,0:T(8,128)S(1)}, u32[]{:S(2)}, u32[]{:S(2)}) collective-permute-start(f32[112,128]{1,0:T(8,128)S(1)} %get-tuple-element.18), channel_id=1, source_target_pairs={{0,2},{1,17},{2,0},{3,19},{16,18},{17,1},{18,16},{19,3},{4,6},{5,2... | collective-permute-start | bytes 172040 | tf_op jit(solution)/shard_map/ppermute | solution.py:18
  12.0 3.3 %collective-permute-start.5 = (bf16[112,128]{1,0:T(8,128)(2,1)S(1)}, bf16[112,128]{1,0:T(8,128)(2,1)S(1)}, u32[]{:S(2)}, u32[]{:S(2)}) collective-permute-start(bf16[112,128]{1,0:T(8,128)(2,1)S(1)} %shard_map.87.refs_3_), channel_id=1, source_target_pairs={{0,3},{1,16},{2,1},{3,18},{16,19},{17,0},{18,17},{19,2},{4,7},{5,2... | collective-permute-start | bytes 86024 | tf_op jit(solution)/shard_map/ppermute | solution.py:18
  12.1 3.9 %collective-permute-start.6 = (bf16[112,128]{1,0:T(8,128)(2,1)S(1)}, bf16[112,128]{1,0:T(8,128)(2,1)S(1)}, u32[]{:S(2)}, u32[]{:S(2)}) collective-permute-start(bf16[112,128]{1,0:T(8,128)(2,1)S(1)} %shard_map.87.refs_3_), channel_id=1, source_target_pairs={{0,2},{1,17},{2,0},{3,19},{16,18},{17,1},{18,16},{19,3},{4,6},{5,2... | collective-permute-start | bytes 86024 | tf_op jit(solution)/shard_map/ppermute | solution.py:18
  12.7 3.3 %collective-permute-start.7 = (bf16[112,128]{1,0:T(8,128)(2,1)S(1)}, bf16[112,128]{1,0:T(8,128)(2,1)S(1)}, u32[]{:S(2)}, u32[]{:S(2)}) collective-permute-start(bf16[112,128]{1,0:T(8,128)(2,1)S(1)} %shard_map.87.refs_3_), channel_id=1, source_target_pairs={{0,1},{1,0},{2,3},{3,2},{16,17},{17,16},{18,19},{19,18},{4,5},{5,4... | collective-permute-start | bytes 86024 | tf_op jit(solution)/shard_map/ppermute | solution.py:18

commit v8 on v3

--- a/solution.py
+++ b/solution.py
@@ -10,6 +10,7 @@
 
 GROUP = ("pair", "dp")
 LANES = 128
+PARTS = 4
 
 
 def send(array, bits, core_1_bits=None):
@@ -105,7 +106,7 @@
 
 
 def order_kernel(own, tiles, *refs):
-    pieces, out_ref, scratch = refs[:4], refs[4], refs[5]
+    pieces, (out_ref, scratch, ready, sems) = refs[:4], refs[4:]
     pair, shard = lax.axis_index("pair"), lax.axis_index("dp")
     core, near = shard & 1, (shard >> 1) & 1
     sources = (
@@ -121,18 +122,26 @@
                 row = ((p ^ (slot * (1 - c))) * 4 + (n ^ (slot * c)) * 2 + c) * own + o
                 start = (slot * own + o) * tiles
                 scratch[row_at(row, tiles, 8 * own), :] = piece[start:start + tiles]
-    out_ref[...] = scratch[...].astype(out_ref.dtype)
-
-
-def call(body, outs, *args, hbm=False, scratch=()):
-    space = pltpu.HBM if hbm else pltpu.VMEM
+    part = scratch.shape[0] // PARTS
+    copies = []
+    for i in range(PARTS):
+        at = pl.ds(i * part, part)
+        ready[at, :] = scratch[at, :].astype(ready.dtype)
+        copies.append(pltpu.make_async_copy(ready.at[at], out_ref.at[at], sems.at[i]))
+        copies[i].start()
+    for copy in copies:
+        copy.wait()
+
+
+def call(body, outs, *args, hbm=False, out_hbm=False, scratch=()):
+    space, out_space = (pltpu.HBM if h else pltpu.VMEM for h in (hbm, out_hbm))
     specs = [pl.BlockSpec(memory_space=pltpu.SMEM if a.dtype == jnp.int32 else space) for a in args]
     held = sum(math.prod(a.shape) * a.dtype.itemsize for a in [*args, *jax.tree.leaves(outs)])
     return pl.pallas_call(
         body,
         out_shape=outs,
         in_specs=specs,
-        out_specs=jax.tree.map(lambda _: pl.BlockSpec(memory_space=pltpu.VMEM), outs),
+        out_specs=jax.tree.map(lambda _: pl.BlockSpec(memory_space=out_space), outs),
         scratch_shapes=list(scratch),
         compiler_params=pltpu.CompilerParams(vmem_limit_bytes=4 * held + (1 << 20)),
     )(*args)
@@ -186,7 +195,9 @@
     block, sub = 8 * own, min(8, 8 * own)
     params = call(
         functools.partial(order_kernel, own, tiles), shaped((block * tiles, LANES), jnp.bfloat16),
-        *pieces, scratch=[pltpu.VMEM((block * tiles, LANES), f32)])
+        *pieces, out_hbm=True, scratch=[
+            pltpu.VMEM((block * tiles, LANES), f32), pltpu.VMEM((block * tiles, LANES), jnp.bfloat16),
+            pltpu.SemaphoreType.DMA((PARTS,))])
     params = params.reshape(block // sub, tiles, sub, LANES).transpose(0, 2, 1, 3).reshape(2, 4 * own, width)
     for bit in far:
         low, got = (shard & bit) == 0, send(params, bit)

time: 16.3 us -> 16.3 us (level)
  no operation moved by 1% of the time
where the time goes in v8:
time: 16.3 us; the launch traced here: 16.1 us
  starting transfers between devices  8.59 us (53%)
  waiting for transfers between devices  3.78 us (23%)
  Pallas kernels  2.43 us (15%)
  between operations  1.31 us (8%)
    ppermute x8, starting transfers between devices, send(): lax.ppermute(array, GROUP, [(i, i ^ flip[i & 1]) for i in range(size)])  8.59 us
    ppermute x8, waiting for transfers between devices, send(): lax.ppermute(array, GROUP, [(i, i ^ flip[i & 1]) for i in range(size)])  3.78 us
    pallas_call x5, Pallas kernels, call(): pl.pallas_call(body, out_shape=outs, in_specs=specs, out_specs=jax.tree.m...  2.43 us
  transfers between devices with their start and end apart: 8, of which 5 were waited for; matrix products, arithmetic and copies ran while one was open for 0% of the time, Pallas kernels for 10%

profile of v8, /device:TPU:0, one launch (start us, length us, event | category | flops | bytes accessed | tf_op | source)
XLA Modules:
  0.0 16.1 jit_solution(4447883787407991093)
XLA Ops:
  0.6 0.5 %collective-permute-start = (f32[448,128]{1,0:T(8,128)}, f32[448,128]{1,0:T(8,128)S(1)}, u32[]{:S(2)}, u32[]{:S(2)}) collective-permute-start(f32[448,128]{1,0:T(8,128)} %bitcast.26), channel_id=1, source_target_pairs={{0,1},{1,0},{2,3},{3,2},{16,17},{17,16},{18,19},{19,18},{4,5},{5,4... | collective-permute-start | bytes 688136 | tf_op jit(solution)/shard_map/ppermute | solution.py:19
  1.1 0.9 %shard_map.84 = (f32[112,1,128]{2,1,0:T(1,128)S(1)}, f32[112,1,128]{2,1,0:T(1,128)S(1)}, f32[168,1,128]{2,1,0:T(1,128)S(1)}) custom-call(f32[56,8,1,128]{3,2,1,0:T(1,128)} %bitcast.27, f32[56,1,128]{2,1,0:T(1,128)} %bitcast.29, f32[56,1,128]{2,1,0:T(1,128)} %bitcast.30, f32[56,1,128]{2,1,0:T(1,128)} %bitcast.31), custom_call_target="tpu_custom_call" | custom-call | tf_op jit(solution)/shard_map/pallas_call | solution.py:140
  2.1 2.6 %collective-permute-start.4 = (f32[168,128]{1,0:T(8,128)S(1)}, f32[168,128]{1,0:T(8,128)S(1)}, u32[]{:S(2)}, u32[]{:S(2)}) collective-permute-start(f32[168,128]{1,0:T(8,128)S(1)} %bitcast.21), channel_id=1, source_target_pairs={{0,16},{1,3},{2,18},{3,1},{16,0},{17,19},{18,2},{19,17},{4,20},{5,... | collective-permute-start | bytes 258056 | tf_op jit(solution)/shard_map/ppermute | solution.py:19
  4.7 0.0 collective-permute-done.theirs
  4.7 1.7 %collective-permute-start.1 = (f32[112,128]{1,0:T(8,128)S(1)}, f32[112,128]{1,0:T(8,128)S(1)}, u32[]{:S(2)}, u32[]{:S(2)}) collective-permute-start(f32[112,128]{1,0:T(8,128)S(1)} %get-tuple-element.16), channel_id=1, source_target_pairs={{0,18},{1,19},{2,16},{3,17},{16,2},{17,3},{18,0},{19,1},{4,22},{5,... | collective-permute-start | bytes 172040 | tf_op jit(solution)/shard_map/ppermute | solution.py:19
  6.4 0.5 %collective-permute-start.2 = (f32[112,128]{1,0:T(8,128)S(1)}, f32[112,128]{1,0:T(8,128)S(1)}, u32[]{:S(2)}, u32[]{:S(2)}) collective-permute-start(f32[112,128]{1,0:T(8,128)S(1)} %get-tuple-element.17), channel_id=1, source_target_pairs={{0,2},{1,17},{2,0},{3,19},{16,18},{17,1},{18,16},{19,3},{4,6},{5,2... | collective-permute-start | bytes 172040 | tf_op jit(solution)/shard_map/ppermute | solution.py:19
  6.9 1.3 %collective-permute-start.3 = (f32[112,128]{1,0:T(8,128)S(1)}, f32[112,128]{1,0:T(8,128)S(1)}, u32[]{:S(2)}, u32[]{:S(2)}) collective-permute-start(f32[112,128]{1,0:T(8,128)S(1)} %get-tuple-element.18), channel_id=1, source_target_pairs={{0,16},{1,3},{2,18},{3,1},{16,0},{17,19},{18,2},{19,17},{4,20},{5,... | collective-permute-start | bytes 172040 | tf_op jit(solution)/shard_map/ppermute | solution.py:19
  8.9 0.0 collective-permute-done.4.theirs_state
  8.9 1.0 %collective-permute-done.1.cross = f32[112,128]{1,0:T(8,128)S(1)} collective-permute-done((f32[112,128]{1,0:T(8,128)S(1)}, f32[112,128]{1,0:T(8,128)S(1)}, u32[]{:S(2)}, u32[]{:S(2)}) %collective-permute-start.1) | collective-permute-done | bytes 57376 | tf_op jit(solution)/shard_map/ppermute | solution.py:19
  9.9 1.0 %collective-permute-done.2.near = f32[112,128]{1,0:T(8,128)S(1)} collective-permute-done((f32[112,128]{1,0:T(8,128)S(1)}, f32[112,128]{1,0:T(8,128)S(1)}, u32[]{:S(2)}, u32[]{:S(2)}) %collective-permute-start.2) | collective-permute-done | bytes 57376 | tf_op jit(solution)/shard_map/ppermute | solution.py:19
  10.9 0.2 %collective-permute-done.3.level = f32[112,128]{1,0:T(8,128)S(1)} collective-permute-done((f32[112,128]{1,0:T(8,128)S(1)}, f32[112,128]{1,0:T(8,128)S(1)}, u32[]{:S(2)}, u32[]{:S(2)}) %collective-permute-start.3) | collective-permute-done | bytes 57376 | tf_op jit(solution)/shard_map/ppermute | solution.py:19
  11.1 0.1 shard_map.87.refs_3_
  11.2 0.3 %collective-permute-start.5 = (bf16[112,128]{1,0:T(8,128)(2,1)S(1)}, bf16[112,128]{1,0:T(8,128)(2,1)S(1)}, u32[]{:S(2)}, u32[]{:S(2)}) collective-permute-start(bf16[112,128]{1,0:T(8,128)(2,1)S(1)} %shard_map.87.refs_3_), channel_id=1, source_target_pairs={{0,3},{1,16},{2,1},{3,18},{16,19},{17,0},{18,17},{19,2},{4,7},{5,2... | collective-permute-start | bytes 86024 | tf_op jit(solution)/shard_map/ppermute | solution.py:19
  11.5 1.3 %collective-permute-start.6 = (bf16[112,128]{1,0:T(8,128)(2,1)S(1)}, bf16[112,128]{1,0:T(8,128)(2,1)S(1)}, u32[]{:S(2)}, u32[]{:S(2)}) collective-permute-start(bf16[112,128]{1,0:T(8,128)(2,1)S(1)} %shard_map.87.refs_3_), channel_id=1, source_target_pairs={{0,2},{1,17},{2,0},{3,19},{16,18},{17,1},{18,16},{19,3},{4,6},{5,2... | collective-permute-start | bytes 86024 | tf_op jit(solution)/shard_map/ppermute | solution.py:19
  12.8 0.3 %collective-permute-start.7 = (bf16[112,128]{1,0:T(8,128)(2,1)S(1)}, bf16[112,128]{1,0:T(8,128)(2,1)S(1)}, u32[]{:S(2)}, u32[]{:S(2)}) collective-permute-start(bf16[112,128]{1,0:T(8,128)(2,1)S(1)} %shard_map.87.refs_3_), channel_id=1, source_target_pairs={{0,1},{1,0},{2,3},{3,2},{16,17},{17,16},{18,19},{19,18},{4,5},{5,4... | collective-permute-start | bytes 86024 | tf_op jit(solution)/shard_map/ppermute | solution.py:19
  13.1 0.7 %shard_map.86 = (f32[56,128]{1,0:T(8,128)}, f32[56,128]{1,0:T(8,128)}, f32[56,128]{1,0:T(8,128)}) custom-call(s32[1]{0:T(128)S(6)} %copy.9.step_ref, f32[112,128]{1,0:T(8,128)S(1)} %collective-permute-done.1.cross, f32[112,128]{1,0:T(8,128)S(1)} %collective-permute-done.2.near, f32[112,128]{1,0:T(8,128)S(1)} %collective-permute-done.3.level, ...), custom_call_target="tpu_custom_call" | custom-call | tf_op jit(solution)/shard_map/pallas_call | solution.py:140
  13.8 0.8 %collective-permute-done.5.refs_0_ = bf16[112,128]{1,0:T(8,128)(2,1)S(1)} collective-permute-done((bf16[112,128]{1,0:T(8,128)(2,1)S(1)}, bf16[112,128]{1,0:T(8,128)(2,1)S(1)}, u32[]{:S(2)}, u32[]{:S(2)}) %collective-permute-start.5) | collective-permute-done | bytes 28704 | tf_op jit(solution)/shard_map/ppermute | solution.py:19
  14.5 0.8 %collective-permute-done.6.refs_1_ = bf16[112,128]{1,0:T(8,128)(2,1)S(1)} collective-permute-done((bf16[112,128]{1,0:T(8,128)(2,1)S(1)}, bf16[112,128]{1,0:T(8,128)(2,1)S(1)}, u32[]{:S(2)}, u32[]{:S(2)}) %collective-permute-start.6) | collective-permute-done | bytes 28704 | tf_op jit(solution)/shard_map/ppermute | solution.py:19
  15.3 0.0 collective-permute-done.7.refs_2_
  15.4 0.8 %shard_map.88 = bf16[448,128]{1,0:T(8,128)(2,1)} custom-call(bf16[112,128]{1,0:T(8,128)(2,1)S(1)} %collective-permute-done.5.refs_0_, bf16[112,128]{1,0:T(8,128)(2,1)S(1)} %collective-permute-done.6.refs_1_, bf16[112,128]{1,0:T(8,128)(2,1)S(1)} %collective-permute-done.7.refs_2_, bf16[112,128]{1,0:T(8,128)(2,1)S(1)} %shard_map.87.refs_3_), custom_call_target="tpu_custom_call" | custom-call | tf_op jit(solution)/shard_map/pallas_call | solution.py:140
  (1 shorter events, 0.0 us)
Async XLA Ops:
  0.6 4.0 %collective-permute-start = (f32[448,128]{1,0:T(8,128)}, f32[448,128]{1,0:T(8,128)S(1)}, u32[]{:S(2)}, u32[]{:S(2)}) collective-permute-start(f32[448,128]{1,0:T(8,128)} %bitcast.26), channel_id=1, source_target_pairs={{0,1},{1,0},{2,3},{3,2},{16,17},{17,16},{18,19},{19,18},{4,5},{5,4... | collective-permute-start | bytes 688136 | tf_op jit(solution)/shard_map/ppermute | solution.py:19
  2.1 6.9 %collective-permute-start.4 = (f32[168,128]{1,0:T(8,128)S(1)}, f32[168,128]{1,0:T(8,128)S(1)}, u32[]{:S(2)}, u32[]{:S(2)}) collective-permute-start(f32[168,128]{1,0:T(8,128)S(1)} %bitcast.21), channel_id=1, source_target_pairs={{0,16},{1,3},{2,18},{3,1},{16,0},{17,19},{18,2},{19,17},{4,20},{5,... | collective-permute-start | bytes 258056 | tf_op jit(solution)/shard_map/ppermute | solution.py:19
  4.7 5.2 %collective-permute-start.1 = (f32[112,128]{1,0:T(8,128)S(1)}, f32[112,128]{1,0:T(8,128)S(1)}, u32[]{:S(2)}, u32[]{:S(2)}) collective-permute-start(f32[112,128]{1,0:T(8,128)S(1)} %get-tuple-element.16), channel_id=1, source_target_pairs={{0,18},{1,19},{2,16},{3,17},{16,2},{17,3},{18,0},{19,1},{4,22},{5,... | collective-permute-start | bytes 172040 | tf_op jit(solution)/shard_map/ppermute | solution.py:19
  6.4 4.5 %collective-permute-start.2 = (f32[112,128]{1,0:T(8,128)S(1)}, f32[112,128]{1,0:T(8,128)S(1)}, u32[]{:S(2)}, u32[]{:S(2)}) collective-permute-start(f32[112,128]{1,0:T(8,128)S(1)} %get-tuple-element.17), channel_id=1, source_target_pairs={{0,2},{1,17},{2,0},{3,19},{16,18},{17,1},{18,16},{19,3},{4,6},{5,2... | collective-permute-start | bytes 172040 | tf_op jit(solution)/shard_map/ppermute | solution.py:19
  6.9 4.2 %collective-permute-start.3 = (f32[112,128]{1,0:T(8,128)S(1)}, f32[112,128]{1,0:T(8,128)S(1)}, u32[]{:S(2)}, u32[]{:S(2)}) collective-permute-start(f32[112,128]{1,0:T(8,128)S(1)} %get-tuple-element.18), channel_id=1, source_target_pairs={{0,16},{1,3},{2,18},{3,1},{16,0},{17,19},{18,2},{19,17},{4,20},{5,... | collective-permute-start | bytes 172040 | tf_op jit(solution)/shard_map/ppermute | solution.py:19
  11.2 3.3 %collective-permute-start.5 = (bf16[112,128]{1,0:T(8,128)(2,1)S(1)}, bf16[112,128]{1,0:T(8,128)(2,1)S(1)}, u32[]{:S(2)}, u32[]{:S(2)}) collective-permute-start(bf16[112,128]{1,0:T(8,128)(2,1)S(1)} %shard_map.87.refs_3_), channel_id=1, source_target_pairs={{0,3},{1,16},{2,1},{3,18},{16,19},{17,0},{18,17},{19,2},{4,7},{5,2... | collective-permute-start | bytes 86024 | tf_op jit(solution)/shard_map/ppermute | solution.py:19
  11.5 3.9 %collective-permute-start.6 = (bf16[112,128]{1,0:T(8,128)(2,1)S(1)}, bf16[112,128]{1,0:T(8,128)(2,1)S(1)}, u32[]{:S(2)}, u32[]{:S(2)}) collective-permute-start(bf16[112,128]{1,0:T(8,128)(2,1)S(1)} %shard_map.87.refs_3_), channel_id=1, source_target_pairs={{0,2},{1,17},{2,0},{3,19},{16,18},{17,1},{18,16},{19,3},{4,6},{5,2... | collective-permute-start | bytes 86024 | tf_op jit(solution)/shard_map/ppermute | solution.py:19
  12.8 2.5 %collective-permute-start.7 = (bf16[112,128]{1,0:T(8,128)(2,1)S(1)}, bf16[112,128]{1,0:T(8,128)(2,1)S(1)}, u32[]{:S(2)}, u32[]{:S(2)}) collective-permute-start(bf16[112,128]{1,0:T(8,128)(2,1)S(1)} %shard_map.87.refs_3_), channel_id=1, source_target_pairs={{0,1},{1,0},{2,3},{3,2},{16,17},{17,16},{18,19},{19,18},{4,5},{5,4... | collective-permute-start | bytes 86024 | tf_op jit(solution)/shard_map/ppermute | solution.py:19

commit v9 on v3

--- a/solution.py
+++ b/solution.py
@@ -44,12 +44,12 @@
 def front_kernel(dims, local, master, moment, second, keep_ref, give_ref, state_ref, sems):
     size, tiles, sub = master.shape[0], dims[2], local.shape[1]
     copies = []
-    for i, source in enumerate((master, moment, second)):
-        copies.append((source, state_ref.at[pl.ds(i * size, size)]))
     for to, rows in my_rows(*dims):
         for row, out_ref in zip(rows, (keep_ref, give_ref)):
             block = pl.ds((row // sub) * tiles, tiles)
             copies.append((local.at[block, row % sub], out_ref.at[to]))
+    for i, source in enumerate((master, moment, second)):
+        copies.append((source, state_ref.at[pl.ds(i * size, size)]))
     copies = [pltpu.make_async_copy(*c, sems.at[i]) for i, c in enumerate(copies)]
     for copy in copies:
         copy.start()

time: 16.3 us -> 16.3 us (level)
  no operation moved by 1% of the time
where the time goes in v9:
time: 16.3 us; the launch traced here: 16.1 us
  starting transfers between devices  8.6 us (53%)
  waiting for transfers between devices  3.76 us (23%)
  Pallas kernels  2.42 us (15%)
  between operations  1.31 us (8%)
    ppermute x8, starting transfers between devices, send(): lax.ppermute(array, GROUP, [(i, i ^ flip[i & 1]) for i in range(size)])  8.6 us
    ppermute x8, waiting for transfers between devices, send(): lax.ppermute(array, GROUP, [(i, i ^ flip[i & 1]) for i in range(size)])  3.76 us
    pallas_call x5, Pallas kernels, call(): pl.pallas_call(body, out_shape=outs, in_specs=specs, out_specs=jax.tree.m...  2.42 us
  transfers between devices with their start and end apart: 8, of which 5 were waited for; matrix products, arithmetic and copies ran while one was open for 0% of the time, Pallas kernels for 10%

profile of v9, /device:TPU:0, one launch (start us, length us, event | category | flops | bytes accessed | tf_op | source)
XLA Modules:
  0.0 16.1 jit_solution(10578686421283177541)
XLA Ops:
  0.6 0.5 %collective-permute-start = (f32[448,128]{1,0:T(8,128)}, f32[448,128]{1,0:T(8,128)S(1)}, u32[]{:S(2)}, u32[]{:S(2)}) collective-permute-start(f32[448,128]{1,0:T(8,128)} %bitcast.26), channel_id=1, source_target_pairs={{0,1},{1,0},{2,3},{3,2},{16,17},{17,16},{18,19},{19,18},{4,5},{5,4... | collective-permute-start | bytes 688136 | tf_op jit(solution)/shard_map/ppermute | solution.py:18
  1.1 0.9 %shard_map.84 = (f32[112,1,128]{2,1,0:T(1,128)S(1)}, f32[112,1,128]{2,1,0:T(1,128)S(1)}, f32[168,1,128]{2,1,0:T(1,128)S(1)}) custom-call(f32[56,8,1,128]{3,2,1,0:T(1,128)} %bitcast.27, f32[56,1,128]{2,1,0:T(1,128)} %bitcast.29, f32[56,1,128]{2,1,0:T(1,128)} %bitcast.30, f32[56,1,128]{2,1,0:T(1,128)} %bitcast.31), custom_call_target="tpu_custom_call" | custom-call | tf_op jit(solution)/shard_map/pallas_call | solution.py:131
  2.1 2.6 %collective-permute-start.4 = (f32[168,128]{1,0:T(8,128)S(1)}, f32[168,128]{1,0:T(8,128)S(1)}, u32[]{:S(2)}, u32[]{:S(2)}) collective-permute-start(f32[168,128]{1,0:T(8,128)S(1)} %bitcast.21), channel_id=1, source_target_pairs={{0,16},{1,3},{2,18},{3,1},{16,0},{17,19},{18,2},{19,17},{4,20},{5,... | collective-permute-start | bytes 258056 | tf_op jit(solution)/shard_map/ppermute | solution.py:18
  4.7 0.0 collective-permute-done.theirs
  4.7 1.7 %collective-permute-start.1 = (f32[112,128]{1,0:T(8,128)S(1)}, f32[112,128]{1,0:T(8,128)S(1)}, u32[]{:S(2)}, u32[]{:S(2)}) collective-permute-start(f32[112,128]{1,0:T(8,128)S(1)} %get-tuple-element.16), channel_id=1, source_target_pairs={{0,18},{1,19},{2,16},{3,17},{16,2},{17,3},{18,0},{19,1},{4,22},{5,... | collective-permute-start | bytes 172040 | tf_op jit(solution)/shard_map/ppermute | solution.py:18
  6.4 0.5 %collective-permute-start.2 = (f32[112,128]{1,0:T(8,128)S(1)}, f32[112,128]{1,0:T(8,128)S(1)}, u32[]{:S(2)}, u32[]{:S(2)}) collective-permute-start(f32[112,128]{1,0:T(8,128)S(1)} %get-tuple-element.17), channel_id=1, source_target_pairs={{0,2},{1,17},{2,0},{3,19},{16,18},{17,1},{18,16},{19,3},{4,6},{5,2... | collective-permute-start | bytes 172040 | tf_op jit(solution)/shard_map/ppermute | solution.py:18
  6.9 1.3 %collective-permute-start.3 = (f32[112,128]{1,0:T(8,128)S(1)}, f32[112,128]{1,0:T(8,128)S(1)}, u32[]{:S(2)}, u32[]{:S(2)}) collective-permute-start(f32[112,128]{1,0:T(8,128)S(1)} %get-tuple-element.18), channel_id=1, source_target_pairs={{0,16},{1,3},{2,18},{3,1},{16,0},{17,19},{18,2},{19,17},{4,20},{5,... | collective-permute-start | bytes 172040 | tf_op jit(solution)/shard_map/ppermute | solution.py:18
  8.9 0.0 collective-permute-done.4.theirs_state
  8.9 1.0 %collective-permute-done.1.cross = f32[112,128]{1,0:T(8,128)S(1)} collective-permute-done((f32[112,128]{1,0:T(8,128)S(1)}, f32[112,128]{1,0:T(8,128)S(1)}, u32[]{:S(2)}, u32[]{:S(2)}) %collective-permute-start.1) | collective-permute-done | bytes 57376 | tf_op jit(solution)/shard_map/ppermute | solution.py:18
  9.9 1.0 %collective-permute-done.2.near = f32[112,128]{1,0:T(8,128)S(1)} collective-permute-done((f32[112,128]{1,0:T(8,128)S(1)}, f32[112,128]{1,0:T(8,128)S(1)}, u32[]{:S(2)}, u32[]{:S(2)}) %collective-permute-start.2) | collective-permute-done | bytes 57376 | tf_op jit(solution)/shard_map/ppermute | solution.py:18
  10.9 0.2 %collective-permute-done.3.level = f32[112,128]{1,0:T(8,128)S(1)} collective-permute-done((f32[112,128]{1,0:T(8,128)S(1)}, f32[112,128]{1,0:T(8,128)S(1)}, u32[]{:S(2)}, u32[]{:S(2)}) %collective-permute-start.3) | collective-permute-done | bytes 57376 | tf_op jit(solution)/shard_map/ppermute | solution.py:18
  11.1 0.1 shard_map.87.refs_3_
  11.2 0.3 %collective-permute-start.5 = (bf16[112,128]{1,0:T(8,128)(2,1)S(1)}, bf16[112,128]{1,0:T(8,128)(2,1)S(1)}, u32[]{:S(2)}, u32[]{:S(2)}) collective-permute-start(bf16[112,128]{1,0:T(8,128)(2,1)S(1)} %shard_map.87.refs_3_), channel_id=1, source_target_pairs={{0,3},{1,16},{2,1},{3,18},{16,19},{17,0},{18,17},{19,2},{4,7},{5,2... | collective-permute-start | bytes 86024 | tf_op jit(solution)/shard_map/ppermute | solution.py:18
  11.5 1.3 %collective-permute-start.6 = (bf16[112,128]{1,0:T(8,128)(2,1)S(1)}, bf16[112,128]{1,0:T(8,128)(2,1)S(1)}, u32[]{:S(2)}, u32[]{:S(2)}) collective-permute-start(bf16[112,128]{1,0:T(8,128)(2,1)S(1)} %shard_map.87.refs_3_), channel_id=1, source_target_pairs={{0,2},{1,17},{2,0},{3,19},{16,18},{17,1},{18,16},{19,3},{4,6},{5,2... | collective-permute-start | bytes 86024 | tf_op jit(solution)/shard_map/ppermute | solution.py:18
  12.8 0.3 %collective-permute-start.7 = (bf16[112,128]{1,0:T(8,128)(2,1)S(1)}, bf16[112,128]{1,0:T(8,128)(2,1)S(1)}, u32[]{:S(2)}, u32[]{:S(2)}) collective-permute-start(bf16[112,128]{1,0:T(8,128)(2,1)S(1)} %shard_map.87.refs_3_), channel_id=1, source_target_pairs={{0,1},{1,0},{2,3},{3,2},{16,17},{17,16},{18,19},{19,18},{4,5},{5,4... | collective-permute-start | bytes 86024 | tf_op jit(solution)/shard_map/ppermute | solution.py:18
  13.1 0.7 %shard_map.86 = (f32[56,128]{1,0:T(8,128)}, f32[56,128]{1,0:T(8,128)}, f32[56,128]{1,0:T(8,128)}) custom-call(s32[1]{0:T(128)S(6)} %copy.9.step_ref, f32[112,128]{1,0:T(8,128)S(1)} %collective-permute-done.1.cross, f32[112,128]{1,0:T(8,128)S(1)} %collective-permute-done.2.near, f32[112,128]{1,0:T(8,128)S(1)} %collective-permute-done.3.level, ...), custom_call_target="tpu_custom_call" | custom-call | tf_op jit(solution)/shard_map/pallas_call | solution.py:131
  13.8 0.8 %collective-permute-done.5.refs_0_ = bf16[112,128]{1,0:T(8,128)(2,1)S(1)} collective-permute-done((bf16[112,128]{1,0:T(8,128)(2,1)S(1)}, bf16[112,128]{1,0:T(8,128)(2,1)S(1)}, u32[]{:S(2)}, u32[]{:S(2)}) %collective-permute-start.5) | collective-permute-done | bytes 28704 | tf_op jit(solution)/shard_map/ppermute | solution.py:18
  14.5 0.8 %collective-permute-done.6.refs_1_ = bf16[112,128]{1,0:T(8,128)(2,1)S(1)} collective-permute-done((bf16[112,128]{1,0:T(8,128)(2,1)S(1)}, bf16[112,128]{1,0:T(8,128)(2,1)S(1)}, u32[]{:S(2)}, u32[]{:S(2)}) %collective-permute-start.6) | collective-permute-done | bytes 28704 | tf_op jit(solution)/shard_map/ppermute | solution.py:18
  15.3 0.0 collective-permute-done.7.refs_2_
  15.4 0.7 %shard_map.88 = bf16[448,128]{1,0:T(8,128)(2,1)} custom-call(bf16[112,128]{1,0:T(8,128)(2,1)S(1)} %collective-permute-done.5.refs_0_, bf16[112,128]{1,0:T(8,128)(2,1)S(1)} %collective-permute-done.6.refs_1_, bf16[112,128]{1,0:T(8,128)(2,1)S(1)} %collective-permute-done.7.refs_2_, bf16[112,128]{1,0:T(8,128)(2,1)S(1)} %shard_map.87.refs_3_), custom_call_target="tpu_custom_call" | custom-call | tf_op jit(solution)/shard_map/pallas_call | solution.py:131
  (1 shorter events, 0.0 us)
Async XLA Ops:
  0.6 4.1 %collective-permute-start = (f32[448,128]{1,0:T(8,128)}, f32[448,128]{1,0:T(8,128)S(1)}, u32[]{:S(2)}, u32[]{:S(2)}) collective-permute-start(f32[448,128]{1,0:T(8,128)} %bitcast.26), channel_id=1, source_target_pairs={{0,1},{1,0},{2,3},{3,2},{16,17},{17,16},{18,19},{19,18},{4,5},{5,4... | collective-permute-start | bytes 688136 | tf_op jit(solution)/shard_map/ppermute | solution.py:18
  2.1 6.9 %collective-permute-start.4 = (f32[168,128]{1,0:T(8,128)S(1)}, f32[168,128]{1,0:T(8,128)S(1)}, u32[]{:S(2)}, u32[]{:S(2)}) collective-permute-start(f32[168,128]{1,0:T(8,128)S(1)} %bitcast.21), channel_id=1, source_target_pairs={{0,16},{1,3},{2,18},{3,1},{16,0},{17,19},{18,2},{19,17},{4,20},{5,... | collective-permute-start | bytes 258056 | tf_op jit(solution)/shard_map/ppermute | solution.py:18
  4.7 5.2 %collective-permute-start.1 = (f32[112,128]{1,0:T(8,128)S(1)}, f32[112,128]{1,0:T(8,128)S(1)}, u32[]{:S(2)}, u32[]{:S(2)}) collective-permute-start(f32[112,128]{1,0:T(8,128)S(1)} %get-tuple-element.16), channel_id=1, source_target_pairs={{0,18},{1,19},{2,16},{3,17},{16,2},{17,3},{18,0},{19,1},{4,22},{5,... | collective-permute-start | bytes 172040 | tf_op jit(solution)/shard_map/ppermute | solution.py:18
  6.4 4.5 %collective-permute-start.2 = (f32[112,128]{1,0:T(8,128)S(1)}, f32[112,128]{1,0:T(8,128)S(1)}, u32[]{:S(2)}, u32[]{:S(2)}) collective-permute-start(f32[112,128]{1,0:T(8,128)S(1)} %get-tuple-element.17), channel_id=1, source_target_pairs={{0,2},{1,17},{2,0},{3,19},{16,18},{17,1},{18,16},{19,3},{4,6},{5,2... | collective-permute-start | bytes 172040 | tf_op jit(solution)/shard_map/ppermute | solution.py:18
  6.9 4.2 %collective-permute-start.3 = (f32[112,128]{1,0:T(8,128)S(1)}, f32[112,128]{1,0:T(8,128)S(1)}, u32[]{:S(2)}, u32[]{:S(2)}) collective-permute-start(f32[112,128]{1,0:T(8,128)S(1)} %get-tuple-element.18), channel_id=1, source_target_pairs={{0,16},{1,3},{2,18},{3,1},{16,0},{17,19},{18,2},{19,17},{4,20},{5,... | collective-permute-start | bytes 172040 | tf_op jit(solution)/shard_map/ppermute | solution.py:18
  11.2 3.3 %collective-permute-start.5 = (bf16[112,128]{1,0:T(8,128)(2,1)S(1)}, bf16[112,128]{1,0:T(8,128)(2,1)S(1)}, u32[]{:S(2)}, u32[]{:S(2)}) collective-permute-start(bf16[112,128]{1,0:T(8,128)(2,1)S(1)} %shard_map.87.refs_3_), channel_id=1, source_target_pairs={{0,3},{1,16},{2,1},{3,18},{16,19},{17,0},{18,17},{19,2},{4,7},{5,2... | collective-permute-start | bytes 86024 | tf_op jit(solution)/shard_map/ppermute | solution.py:18
  11.5 3.9 %collective-permute-start.6 = (bf16[112,128]{1,0:T(8,128)(2,1)S(1)}, bf16[112,128]{1,0:T(8,128)(2,1)S(1)}, u32[]{:S(2)}, u32[]{:S(2)}) collective-permute-start(bf16[112,128]{1,0:T(8,128)(2,1)S(1)} %shard_map.87.refs_3_), channel_id=1, source_target_pairs={{0,2},{1,17},{2,0},{3,19},{16,18},{17,1},{18,16},{19,3},{4,6},{5,2... | collective-permute-start | bytes 86024 | tf_op jit(solution)/shard_map/ppermute | solution.py:18
  12.8 2.5 %collective-permute-start.7 = (bf16[112,128]{1,0:T(8,128)(2,1)S(1)}, bf16[112,128]{1,0:T(8,128)(2,1)S(1)}, u32[]{:S(2)}, u32[]{:S(2)}) collective-permute-start(bf16[112,128]{1,0:T(8,128)(2,1)S(1)} %shard_map.87.refs_3_), channel_id=1, source_target_pairs={{0,1},{1,0},{2,3},{3,2},{16,17},{17,16},{18,19},{19,18},{4,5},{5,4... | collective-permute-start | bytes 86024 | tf_op jit(solution)/shard_map/ppermute | solution.py:18
